TPU v7x, 256 devices: a whole 4x4x8 slice. The times are simulated.
256 devices in a mesh: dp: 32 (over z_hi, x, core), node: 8 (over y, z_lo).
Axes of the slice: x: 4, y: 4, z: 8 (z_hi: 4, z_lo: 2; z = z_hi * 2 + z_lo), core: 2. Of those that a mesh axis runs over, the one named last changes fastest.
Arguments:
- x_band: bfloat16 [32768, 512], P(('dp', 'node')), may hold values from -6 to 6
- d_gate_up: bfloat16 [32768, 18432], P(('dp', 'node')), may hold values from -0.125 to 0.125
- owner: int32 [36], replicated, may hold values from 0 to 31, as said below
- stat_left: float32 [32, 2, 512, 512], P('dp', None, 'node'), as said below
- stat_right: float32 [32, 2, 512, 512], P('dp', None, 'node'), as said below
Outputs:
- directions: bfloat16 [512, 18432], P('node')
- stat_left_new: float32 [32, 2, 512, 512], P('dp', None, 'node')
- stat_right_new: float32 [32, 2, 512, 512], P('dp', None, 'node')
Inputs may be any that keep to these rules, and one draw needn't show every extreme that they name: owner[0], ..., owner[31] name every index of dp once, and owner[b] = owner[b - 32] for b >= 32; block b sits in slot b // 32 of its owner. Each stat_left[o, s] is symmetric positive definite. Each stat_right[o, s] is symmetric positive definite.
All inputs are finite; a program needn't handle non-finite values.
Results may differ from a plain program's by a relative error of at most 0.023.
Values may be sent and summed in bfloat16 or wider, within the bound.
No kernel may reach another device: no remote copies, remote signals or barrier semaphores. Data moves between devices by JAX's collectives and lax.ppermute only.
A program may use at most 128 MiB of HBM per device.

v0:
```python
import functools
import math

import jax
import jax.numpy as jnp
import numpy as np
from jax import lax
from jax.experimental import pallas as pl
from jax.experimental.pallas import tpu as pltpu
from jax.sharding import Mesh, PartitionSpec as P

B = 512
SLOTS = 2
BETA = 0.9
EXTRA_CHUNK = 128
FLOW = B + EXTRA_CHUNK
HALF = B // 2

FINE = ("z_hi", "x", "core", "y", "z_lo")
FINE_SIZES = (4, 4, 2, 4, 2)
VMEM_LIMIT = 24 * 1024 * 1024

COEF = [6.25 / 4, -(1.25 + 1.25**5) / 4] + [
    -math.comb(5, k) * 1.25 ** (5 - k) * (-0.25) ** k / 4 for k in range(1, 6)
]

ANY = pl.BlockSpec(memory_space=pl.ANY)
HBM = pl.BlockSpec(memory_space=pltpu.HBM)
SMEM = pl.BlockSpec(memory_space=pltpu.SMEM)
VMEM = pl.BlockSpec(memory_space=pltpu.VMEM)
PARAMS = pltpu.CompilerParams(vmem_limit_bytes=VMEM_LIMIT)


def swap(value, axis, mask):
    size = FINE_SIZES[FINE.index(axis)]
    return lax.ppermute(value, axis, [(i, i ^ mask) for i in range(size)])


def aligned(index, step):
    return pl.multiple_of(index * step, step)


def fill_positions(place, position):
    for block in range(32):
        position[place[len(FINE) + block]] = block


X_DIRECT = 4 * FLOW
X_MSG = 6 * FLOW + B
Y_DIRECT = 4 * B
Y_MSG = 6 * B + B
OWN_MSG = 4 * FLOW + 4 * B
X_FWD = slice(X_DIRECT, 6 * FLOW + HALF)
Y_FWD = slice(Y_DIRECT, 6 * B + HALF)


class Packer:
    def __init__(self, place, d, position, sem):
        fill_positions(place, position)
        self.position, self.place, self.d, self.sem = position, place, d, sem
        self.cores = (place[2], 1 - place[2])
        self.copies = []

    def copy(self, source, first, width, target, at):
        self.copies.append(
            pltpu.make_async_copy(source.at[:, pl.ds(first, width)], target.at[:, pl.ds(at, width)], self.sem)
        )
        self.copies[-1].start()

    def flow_x(self, flow, r, core, target, at):
        to_x = self.place[1] ^ r
        block = self.position[(flow * 4 + to_x) * 2 + core]
        self.copy(self.d, aligned(block, B), B, target, at)
        chunk = 32 * B // EXTRA_CHUNK + flow * 8 + to_x * 2 + core
        self.copy(self.d, aligned(chunk, EXTRA_CHUNK), EXTRA_CHUNK, target, at + B)

    def flow_y(self, flow, r, core, target, at):
        to_y = self.place[3] ^ r
        for q in range(4):
            block = self.position[(flow * 4 + (self.place[1] ^ q)) * 2 + core]
            self.copy(self.d, pl.multiple_of(block * B + to_y * 128, 128), 128, target, at + q * 128)

    def finish(self):
        for c in self.copies:
            c.wait()


NEIGHBOURS = ((1, 0), (3, 1))


def pack_x_kernel(place, d, xb, x1, x3, position, sem):
    packer = Packer(place, d, position, sem)
    for (near, through), out in zip(NEIGHBOURS, (x1, x3)):
        for i, core in enumerate(packer.cores):
            packer.flow_x(0, near, core, out, i * 2 * FLOW)
            packer.flow_x(1, near, core, out, i * 2 * FLOW + FLOW)
            packer.flow_x(through, 2, core, out, X_DIRECT + i * FLOW)
        for i, h in enumerate((through, 1 - through)):
            packer.copy(xb, h * HALF, HALF, out, 6 * FLOW + i * HALF)
    packer.finish()


def pack_y_kernel(place, d, xb, y1, y3, position, sem):
    packer = Packer(place, d, position, sem)
    for (near, through), out in zip(NEIGHBOURS, (y1, y3)):
        for i, core in enumerate(packer.cores):
            packer.flow_y(2, near, core, out, i * 2 * B)
            packer.flow_y(3, near, core, out, i * 2 * B + B)
            packer.flow_y(2 + through, 2, core, out, Y_DIRECT + i * B)
        for i, h in enumerate((through, 1 - through)):
            packer.copy(xb, h * HALF, HALF, out, 6 * B + i * HALF)
    packer.finish()


def pack_own_kernel(place, d, out, position, sem):
    packer = Packer(place, d, position, sem)
    for i, core in enumerate(packer.cores):
        for flow in range(2):
            packer.flow_x(flow, 0, core, out, (i * 2 + flow) * FLOW)
            packer.flow_y(2 + flow, 0, core, out, 4 * FLOW + (i * 2 + flow) * B)
    packer.finish()


PACK_PARAMS = pltpu.CompilerParams(vmem_limit_bytes=50 * 1024 * 1024)


def packed(kernel, name, widths, place, d, *more):
    rows = d.shape[0]
    return pl.pallas_call(
        kernel,
        out_shape=[jax.ShapeDtypeStruct((rows, w), jnp.bfloat16) for w in widths],
        in_specs=[SMEM, HBM] + [ANY] * len(more),
        out_specs=[VMEM] * len(widths),
        scratch_shapes=[pltpu.SMEM((32,), jnp.int32), pltpu.SemaphoreType.DMA],
        compiler_params=PACK_PARAMS,
        name=name,
    )(place, d, *more)


def contract_rows(a, b):
    return lax.dot_general(a, b, (((0,), (0,)), ((), ())), preferred_element_type=jnp.float32)


def partial_kernel(which, width, own_at, own, xb, near1, near3, far1, far3, out, xs, ds):
    t = own.shape[0]
    keep = 2 * width
    at = which * keep
    rows = pl.ds(0, t)
    xs[rows, :] = xb[...]
    ds[rows, :] = own[:, own_at + at : own_at + at + keep]
    for i, ref in enumerate((near1, near3)):
        rows = pl.ds((1 + i) * t, t)
        ds[rows, :] = ref[:, at : at + keep]
        for k, h in enumerate((i, 1 - i)):
            xs[rows, h * HALF : (h + 1) * HALF] = ref[:, 6 * width + k * HALF : 6 * width + (k + 1) * HALF]
    rows = pl.ds(3 * t, t)
    for i, ref in enumerate((far1, far3)):
        ds[rows, i * width : (i + 1) * width] = ref[:, which * width : (which + 1) * width]
        xs[rows, i * HALF : (i + 1) * HALF] = ref[:, 2 * width :]
    out[...] = contract_rows(xs[...], ds[...]).astype(out.dtype)


def partials(which, width, own_at, pieces):
    t = pieces[0].shape[0]
    return pl.pallas_call(
        functools.partial(partial_kernel, which, width, own_at),
        out_shape=jax.ShapeDtypeStruct((B, 2 * width), jnp.bfloat16),
        in_specs=[VMEM] * len(pieces),
        out_specs=VMEM,
        scratch_shapes=[pltpu.VMEM((4 * t, B), jnp.bfloat16), pltpu.VMEM((4 * t, 2 * width), jnp.bfloat16)],
        compiler_params=PARAMS,
        name="partials",
    )(*pieces)


def wide_sum_kernel(place, near, far, *outs):
    for s, ref in enumerate(outs):
        rows = pl.ds(aligned(place[3] ^ s, 128), 128)
        ref[...] = (near[rows, :].astype(jnp.float32) + far[rows, :].astype(jnp.float32)).astype(ref.dtype)


def tall_sum_kernel(place, near, far, *outs):
    for q, ref in enumerate(outs):
        for flow in range(2):
            at = slice(flow * B + q * 128, flow * B + (q + 1) * 128)
            ref[:, flow * 128 : (flow + 1) * 128] = (
                near[:, at].astype(jnp.float32) + far[:, at].astype(jnp.float32)
            ).astype(ref.dtype)


def chip_sum(kernel, name, shape, place, near, far):
    return pl.pallas_call(
        kernel,
        out_shape=[jax.ShapeDtypeStruct(shape, k) for k in [jnp.float32] + [jnp.bfloat16] * 3],
        in_specs=[SMEM] + [VMEM] * 2,
        out_specs=[VMEM] * 4,
        compiler_params=PARAMS,
        name=name,
    )(place, near, far)


PIECE = 96


def ring_sum_kernel(ry1, rx1, ry3, rx3, ry2, rx2, py0, px0, out):
    wide = py0[...] + ry1[...].astype(jnp.float32) + ry2[...].astype(jnp.float32) + ry3[...].astype(jnp.float32)
    tall = px0[...] + rx1[...].astype(jnp.float32) + rx2[...].astype(jnp.float32) + rx3[...].astype(jnp.float32)
    wide = wide.astype(jnp.bfloat16)
    tall = tall.astype(jnp.bfloat16)
    for z in range(4):
        for low in range(2):
            first = (z * 2 + low) * PIECE
            if z < 2:
                out[first : first + 64, :] = wide[low * 64 : low * 64 + 64, z * FLOW : z * FLOW + B]
            else:
                for g in range(4):
                    from_row = low * 256 + g * 64
                    out[first : first + 64, g * 128 : (g + 1) * 128] = tall[
                        from_row : from_row + 64, (z - 2) * 128 : (z - 1) * 128
                    ]
            for h in range(2):
                for flow in range(2):
                    k = low * 64 + h * 32
                    at = h * 256 + flow * 128
                    out[first + 64 : first + PIECE, at : at + 128] = wide[
                        k : k + 32, flow * FLOW + B : (flow + 1) * FLOW
                    ]


def ring_sum(parts):
    return pl.pallas_call(
        ring_sum_kernel,
        out_shape=jax.ShapeDtypeStruct((8 * PIECE, B), jnp.bfloat16),
        in_specs=[VMEM] * 8,
        out_specs=VMEM,
        compiler_params=PARAMS,
        name="ring_sum",
    )(*parts)


def line_sum_kernel(arrived, out):
    total = arrived[0].astype(jnp.float32)
    for i in range(1, 8):
        total = total + arrived[i].astype(jnp.float32)
    out[...] = total.astype(jnp.bfloat16)


def line_sum(arrived):
    return pl.pallas_call(
        line_sum_kernel,
        out_shape=jax.ShapeDtypeStruct((PIECE, B), jnp.bfloat16),
        in_specs=[VMEM],
        out_specs=VMEM,
        compiler_params=PARAMS,
        name="line_sum",
    )(arrived)


def choose_kernel(place, q0, q1, q2, q3, out, position, held):
    fill_positions(place, position)
    my_x, my_core, my_low = place[1], place[2], place[4]
    mine = position[(place[0] * 4 + my_x) * 2 + my_core]

    @pl.when(mine >= 4)
    def _():
        out[...] = jnp.zeros(out.shape, jnp.bfloat16)

    @pl.when(mine < 4)
    def _():
        for r, ref in enumerate((q0, q1, q2, q3)):
            held[my_x ^ r] = ref[...]
        flow = mine >> 1
        for xl in range(2):
            at_x = 2 * (mine & 1) + xl
            for flip in range(2):
                to = aligned(xl * 2 + (my_core ^ flip), 128)
                for w in range(2):
                    for h in range(2):
                        rows = pl.ds(pl.multiple_of((my_low ^ w) * 64 + h * 32, 32), 32)
                        from_row = (flip * 2 + w) * 32
                        out[rows, pl.ds(to, 128)] = held[
                            at_x, from_row : from_row + 32, pl.ds(aligned(h * 2 + flow, 128), 128)
                        ]


def choose(place, pieces):
    return pl.pallas_call(
        choose_kernel,
        out_shape=jax.ShapeDtypeStruct((128, B), jnp.bfloat16),
        in_specs=[SMEM] + [VMEM] * 4,
        out_specs=VMEM,
        scratch_shapes=[pltpu.SMEM((32,), jnp.int32), pltpu.VMEM((4, 128, B), jnp.bfloat16)],
        compiler_params=PARAMS,
        name="choose",
    )(place, *pieces)


def cast_kernel(left, right, out):
    out[:SLOTS] = left[...].astype(jnp.bfloat16)
    out[SLOTS:] = right[...].astype(jnp.bfloat16)


def cast_rows(left, right):
    return pl.pallas_call(
        cast_kernel,
        out_shape=jax.ShapeDtypeStruct((2 * SLOTS, 64, B), jnp.bfloat16),
        in_specs=[VMEM] * 2,
        out_specs=VMEM,
        compiler_params=PARAMS,
        name="cast_rows",
    )(left, right)


def whole_kernel(place, s0, s1, s2, s3, out):
    for r, piece in enumerate((s0, s1, s2, s3)):
        for w in range(2):
            rows = pl.ds(aligned((place[3] ^ r) * 2 + (place[4] ^ w), 64), 64)
            for k in range(2 * SLOTS):
                out[k, rows, :] = piece[w * 2 * SLOTS + k]


def whole(place, pieces):
    return pl.pallas_call(
        whole_kernel,
        out_shape=jax.ShapeDtypeStruct((2 * SLOTS, B, B), jnp.bfloat16),
        in_specs=[SMEM] + [VMEM] * 4,
        out_specs=VMEM,
        compiler_params=PARAMS,
        name="whole",
    )(place, *pieces)


def root_kernel(slot, place, r0, r1, r2, r3, statistics, left_rows, right_rows, *refs):
    if slot:
        left_first, right_first, directions, left_new, right_new, g_ref, a_ref, m_ref = refs
        left_new[0] = left_first[...]
        right_new[0] = right_first[...]
    else:
        directions, left_new, right_new, g_ref, a_ref, m_ref = refs
    my_z, my_y, my_low = place[0], place[3], place[4]
    node = my_y * 2 + my_low
    first_row = aligned(node, 64)
    for r, piece in enumerate((r0, r1, r2, r3)):
        at_y = my_y ^ r
        if slot:
            g_ref[pl.ds(aligned(at_y, 128), 128), :] = piece[...]
            continue
        for w in range(2):
            at_low = my_low ^ w
            base = w * 64

            @pl.when(my_z < 2)
            def _():
                g_ref[pl.ds(pl.multiple_of(at_y * 128 + at_low * 64, 64), 64), :] = piece[base : base + 64, :]

            @pl.when(my_z >= 2)
            def _():
                for g in range(4):
                    g_ref[
                        pl.ds(pl.multiple_of(at_low * 256 + g * 64, 64), 64),
                        pl.ds(aligned(at_y, 128), 128),
                    ] = piece[base : base + 64, g * 128 : (g + 1) * 128]

    def scaled(gram, old_rows, new_rows, which):
        a_ref[which] = gram
        rows = BETA * old_rows[slot] + a_ref[which, pl.ds(first_row, 64), :] * (1.0 / B)
        if slot:
            new_rows[slot] = rows
        else:
            new_rows[...] = rows
        full = BETA * statistics[which * SLOTS + slot].astype(jnp.float32) + gram * (1.0 / B)
        norm = B * jnp.sqrt(jnp.sum(full * full, keepdims=True) * (1.0 / (B * B)) + 1e-06)
        matrix = full / norm
        a_ref[which] = matrix
        m_ref[which] = matrix.astype(jnp.bfloat16)
        return lax.rsqrt(jnp.sqrt(norm))

    g = g_ref[...]
    left_gram = lax.dot_general(g, g, (((1,), (1,)), ((), ())), preferred_element_type=jnp.float32)
    right_gram = contract_rows(g, g)
    left_scale = scaled(left_gram, left_rows, left_new, 0)
    right_scale = scaled(right_gram, right_rows, right_new, 1)
    power = a_ref[0, pl.ds(first_row, 64), :]
    column = lax.broadcasted_iota(jnp.int32, (64, B), 1)
    row = lax.broadcasted_iota(jnp.int32, (64, B), 0) + first_row
    total = jnp.where(row == column, COEF[0], 0.0) + COEF[1] * power
    for k in range(2, 7):
        power = jnp.dot(power.astype(jnp.bfloat16), m_ref[0], preferred_element_type=jnp.float32)
        total = total + COEF[k] * power
    root = (total * left_scale).astype(jnp.bfloat16)
    half = jnp.dot(root, g, preferred_element_type=jnp.float32).astype(jnp.bfloat16)
    power = half.astype(jnp.float32)
    total = COEF[0] * power
    for k in range(1, 7):
        power = jnp.dot(power.astype(jnp.bfloat16), m_ref[1], preferred_element_type=jnp.float32)
        total = total + COEF[k] * power
    directions[...] = (total * right_scale).astype(jnp.bfloat16)


def roots(slot, place, pieces, statistics, left_rows, right_rows, *first):
    new = jax.ShapeDtypeStruct((SLOTS, 64, B) if slot else (64, B), jnp.float32)
    return pl.pallas_call(
        functools.partial(root_kernel, slot),
        out_shape=[jax.ShapeDtypeStruct((64, B), jnp.bfloat16), new, new],
        in_specs=[SMEM] + [VMEM] * (7 + len(first)),
        out_specs=[VMEM] * 3,
        scratch_shapes=[
            pltpu.VMEM((B, B), jnp.bfloat16),
            pltpu.VMEM((2, B, B), jnp.float32),
            pltpu.VMEM((2, B, B), jnp.bfloat16),
        ],
        compiler_params=PARAMS,
        name="roots",
    )(place, *pieces, statistics, left_rows, right_rows, *first)


def place_kernel(place, *refs):
    sources, out, position, sem = refs[:10], refs[10], refs[11], refs[12]
    fill_positions(place, position)
    my_z, my_x, my_core = place[0], place[1], place[2]

    def find(slot, r, a, held, near1, near3, low, high):
        if r == 0:
            return held, slot * 3 * 4 + a
        if slot == 0 and r == 2:
            return (near3, 4 + a) if a < 2 else (near1, 2 + a)
        if slot == 0:
            return held, (1 if r == 1 else 2) * 4 + a
        if r == 2:
            return (low, a) if a < 2 else (high, a - 2)
        return (near1 if r == 1 else near3), a

    for wait in (False, True):
        for slot in range(SLOTS):
            for flip in range(2):
                for r in range(4):
                    for a in range(4):
                        source, row = find(slot, r, a, *sources[flip * 5 : flip * 5 + 5])
                        block = position[((my_z ^ a) * 4 + (my_x ^ r)) * 2 + (my_core ^ flip)]
                        copy = pltpu.make_async_copy(
                            source.at[pl.ds(row * 64, 64), :],
                            out.at[:, pl.ds(aligned(jnp.minimum(block + slot * 32, 35), B), B)],
                            sem,
                        )
                        act = copy.wait if wait else copy.start
                        if slot == 0:
                            act()
                        else:
                            pl.when(block < 4)(act)


def put_blocks(place, sources, blocks):
    return pl.pallas_call(
        place_kernel,
        out_shape=jax.ShapeDtypeStruct((64, blocks * B), jnp.bfloat16),
        in_specs=[SMEM] + [ANY] * 10,
        out_specs=ANY,
        scratch_shapes=[pltpu.SMEM((32,), jnp.int32), pltpu.SemaphoreType.DMA],
        compiler_params=PARAMS,
        name="put_blocks",
    )(place, *sources)


def around_z(rows):
    a2, a1, a3 = swap(rows, "z_hi", 2), swap(rows, "z_hi", 1), swap(rows, "z_hi", 3)
    return jnp.concatenate([rows, a1, a2, a3])


def shards(x_band, d_gate_up, owner, stat_left, stat_right):
    place = jnp.concatenate([jnp.stack([lax.axis_index(a) for a in FINE]).astype(jnp.int32), owner])
    bucket = d_gate_up.shape[1] // B

    x1, x3 = packed(pack_x_kernel, "pack_x", [X_MSG] * 2, place, d_gate_up, x_band)
    x1, x3 = swap(x1, "x", 1), swap(x3, "x", 3)
    y1, y3 = packed(pack_y_kernel, "pack_y", [Y_MSG] * 2, place, d_gate_up, x_band)
    y1, y3 = swap(y1, "y", 1), swap(y3, "y", 3)
    (own,) = packed(pack_own_kernel, "pack_own", [OWN_MSG], place, d_gate_up)
    statistics = cast_rows(stat_left[0], stat_right[0])
    statistics = jnp.concatenate([statistics, swap(statistics, "z_lo", 1)])
    f0, f1 = swap(x1[:, X_FWD], "x", 3), swap(x3[:, X_FWD], "x", 1)
    y1_on, y3_on, statistics = lax.optimization_barrier((y1[:, Y_FWD], y3[:, Y_FWD], statistics))
    f2, f3 = swap(y1_on, "y", 3), swap(y3_on, "y", 1)
    on_x, on_y = (own, x_band, x1, x3, f0, f1), (own, x_band, y1, y3, f2, f3)
    far_wide = swap(partials(1, FLOW, 0, on_x), "core", 1)
    far_tall = swap(partials(1, B, 4 * FLOW, on_y), "core", 1)
    wide, tall = partials(0, FLOW, 0, on_x), partials(0, B, 4 * FLOW, on_y)
    py0, py1, py2, py3 = chip_sum(wide_sum_kernel, "wide_sum", (128, 2 * FLOW), place, wide, far_wide)
    px0, px1, px2, px3 = chip_sum(tall_sum_kernel, "tall_sum", (B, 256), place, tall, far_tall)
    ry1, rx1 = swap(py1, "y", 1), swap(px1, "x", 1)
    ry3, rx3 = swap(py3, "y", 3), swap(px3, "x", 3)
    ry2, rx2 = swap(py2, "y", 2), swap(px2, "x", 2)
    message = ring_sum((ry1, rx1, ry3, rx3, ry2, rx2, py0, px0))

    message, statistics = lax.optimization_barrier((message, statistics))
    s2, s1, s3 = swap(statistics, "y", 2), swap(statistics, "y", 1), swap(statistics, "y", 3)
    message = lax.all_to_all(message, ("z_hi", "z_lo"), 0, 0, tiled=True)
    line = line_sum(message.reshape(8, PIECE, B))

    main, extra = line[:64], line[64:]
    far = swap(line, "z_lo", 1)
    extra_core = swap(extra, "core", 1)
    diagonal = [(c * 2 + w, 3 - (c * 2 + w)) for c in range(2) for w in range(2)]
    extra_far = lax.ppermute(extra, ("core", "z_lo"), diagonal)
    far, s1, s2, s3 = lax.optimization_barrier((far, s1, s2, s3))
    statistics = whole(place, (statistics, s1, s2, s3))
    m0 = jnp.concatenate([main, far[:64]])
    m2, m1, m3 = swap(m0, "y", 2), swap(m0, "y", 1), swap(m0, "y", 3)
    q0 = jnp.concatenate([extra, far[64:], extra_core, extra_far])
    q2, q1, q3 = swap(q0, "x", 2), swap(q0, "x", 1), swap(q0, "x", 3)
    first, left_first, right_first = roots(0, place, (m0, m1, m2, m3), statistics, stat_left[0], stat_right[0])
    e0 = choose(place, (q0, q1, q2, q3))
    e2, e1, e3 = swap(e0, "y", 2), swap(e0, "y", 1), swap(e0, "y", 3)
    plane, e1, e2, e3 = lax.optimization_barrier((around_z(first), e1, e2, e3))
    second, left_new, right_new = roots(
        1, place, (e0, e1, e2, e3), statistics, stat_left[0], stat_right[0], left_first, right_first
    )
    _, second = lax.optimization_barrier((plane, second))
    first1, first3 = swap(plane, "x", 1), swap(plane, "x", 3)
    second = around_z(second)
    near1 = swap(jnp.concatenate([second, first3[128:]]), "x", 1)
    near3 = swap(jnp.concatenate([second, first1[:128]]), "x", 3)
    held = jnp.concatenate([plane, first1, first3, second])
    sources = (held, near1, near3, swap(near1[:128], "x", 3), swap(near3[128:256], "x", 1))
    out = put_blocks(place, sources + tuple(swap(v, "core", 1) for v in sources), bucket)
    return (out, left_new[None], right_new[None])


def solution(mesh):
    fine = Mesh(np.asarray(mesh.devices).reshape(FINE_SIZES), FINE)
    dp, node = FINE[:3], FINE[3:]
    placed = (P(dp + node, None), P(dp + node, None), P(), P(dp, None, node, None), P(dp, None, node, None))
    return jax.shard_map(
        shards,
        mesh=fine,
        in_specs=placed,
        out_specs=(P(node, None), P(dp, None, node, None), P(dp, None, node, None)),
        check_vma=False,
    )
```

profile of v0, /device:TPU:1, one launch (start us, length us, event | category | flops | bytes accessed | tf_op | source)
XLA Modules:
  0.0 186.9 jit_solution(16594125193750433427)
XLA Ops:
  2.3 2.2 %pack_x.1 = (bf16[128,4352]{1,0:T(8,128)(2,1)S(1)}, bf16[128,4352]{1,0:T(8,128)(2,1)S(1)}) custom-call(s32[41]{0:T(128)S(1)} %concatenate.28.place, bf16[128,18432]{1,0:T(8,128)(2,1)} %d.5, bf16[128,512]{1,0:T(8,128)(2,1)S(1)} %copy-done), custom_call_target="tpu_custom_call" | custom-call | tf_op jit(solution)/shard_map/pack_x/pallas_call | solution.py:129
  4.5 2.1 %collective-permute-start = (bf16[128,4352]{1,0:T(8,128)(2,1)S(1)}, bf16[128,4352]{1,0:T(8,128)(2,1)S(1)}, u32[]{:S(2)}, u32[]{:S(2)}) collective-permute-start(bf16[128,4352]{1,0:T(8,128)(2,1)S(1)} %get-tuple-element.35), channel_id=1, source_target_pairs={{0,16},{16,0},{32,48},{48,32},{1,17},{17,1},{33,49},{49,33},{2,18}... | collective-permute-start | bytes 3342344 | tf_op jit(solution)/shard_map/ppermute | solution.py:36
  6.6 1.8 collective-permute-start.1
  8.4 2.0 %pack_y.1 = (bf16[128,3584]{1,0:T(8,128)(2,1)S(1)}, bf16[128,3584]{1,0:T(8,128)(2,1)S(1)}) custom-call(s32[41]{0:T(128)S(1)} %concatenate.28.place, bf16[128,18432]{1,0:T(8,128)(2,1)} %d.5, bf16[128,512]{1,0:T(8,128)(2,1)S(1)} %copy-done), custom_call_target="tpu_custom_call" | custom-call | tf_op jit(solution)/shard_map/pack_y/pallas_call | solution.py:129
  10.4 1.4 collective-permute-start.6
  11.8 1.9 %collective-permute-start.7 = (bf16[128,3584]{1,0:T(8,128)(2,1)S(1)}, bf16[128,3584]{1,0:T(8,128)(2,1)S(1)}, u32[]{:S(2)}, u32[]{:S(2)}) collective-permute-start(bf16[128,3584]{1,0:T(8,128)(2,1)S(1)} %get-tuple-element.39), channel_id=1, source_target_pairs={{0,6},{2,4},{4,2},{6,0},{1,7},{3,5},{5,3},{7,1},{8,14},{10,12},{12... | collective-permute-start | bytes 2752520 | tf_op jit(solution)/shard_map/ppermute | solution.py:36
  13.7 1.7 collective-permute-start.8
  15.5 14.1 %collective-permute-done.near1 = bf16[128,4352]{1,0:T(8,128)(2,1)S(1)} collective-permute-done((bf16[128,4352]{1,0:T(8,128)(2,1)S(1)}, bf16[128,4352]{1,0:T(8,128)(2,1)S(1)}, u32[]{:S(2)}, u32[]{:S(2)}) %collective-permute-start) | collective-permute-done | bytes 1114144 | tf_op jit(solution)/shard_map/ppermute | solution.py:36
  29.6 3.8 %collective-permute-start.2 = (bf16[128,1536]{1,0:T(8,128)(2,1)S(1)}, bf16[128,1536]{1,0:T(8,128)(2,1)S(1)}, u32[]{:S(2)}, u32[]{:S(2)}) collective-permute-start(bf16[128,1536]{1,0:T(8,128)(2,1)S(1)} %slice.48), channel_id=1, source_target_pairs={{0,48},{16,32},{32,16},{48,0},{1,49},{17,33},{33,17},{49,1},{2,50}... | collective-permute-start | bytes 1179656 | tf_op jit(solution)/shard_map/ppermute | solution.py:36
  33.7 2.8 %collective-permute-start.9 = (bf16[128,1280]{1,0:T(8,128)(2,1)S(1)}, bf16[128,1280]{1,0:T(8,128)(2,1)S(1)}, u32[]{:S(2)}, u32[]{:S(2)}) collective-permute-start(bf16[128,1280]{1,0:T(8,128)(2,1)S(1)} %slice.50), channel_id=1, source_target_pairs={{0,6},{2,4},{4,2},{6,0},{1,7},{3,5},{5,3},{7,1},{8,14},{10,12},{12... | collective-permute-start | bytes 983048 | tf_op jit(solution)/shard_map/ppermute | solution.py:36
  36.5 1.9 %pack_own.1.own = bf16[128,4608]{1,0:T(8,128)(2,1)S(1)} custom-call(s32[41]{0:T(128)S(1)} %concatenate.28.place, bf16[128,18432]{1,0:T(8,128)(2,1)} %d.5), custom_call_target="tpu_custom_call" | custom-call | tf_op jit(solution)/shard_map/pack_own/pallas_call | solution.py:129
  38.5 2.6 %collective-permute-done.2.far1 = bf16[128,1536]{1,0:T(8,128)(2,1)S(1)} collective-permute-done((bf16[128,1536]{1,0:T(8,128)(2,1)S(1)}, bf16[128,1536]{1,0:T(8,128)(2,1)S(1)}, u32[]{:S(2)}, u32[]{:S(2)}) %collective-permute-start.2) | collective-permute-done | bytes 393248 | tf_op jit(solution)/shard_map/ppermute | solution.py:36
  41.1 1.2 collective-permute-done.3.far3
  43.2 2.8 %collective-permute-start.4 = (bf16[512,1280]{1,0:T(8,128)(2,1)S(1)}, bf16[512,1280]{1,0:T(8,128)(2,1)S(1)}, u32[]{:S(2)}, u32[]{:S(2)}) collective-permute-start(bf16[512,1280]{1,0:T(8,128)(2,1)S(1)} %partials.5), channel_id=1, source_target_pairs={{0,8},{8,0},{1,9},{9,1},{2,10},{10,2},{3,11},{11,3},{4,12},{12,4},... | collective-permute-start | bytes 3932168 | tf_op jit(solution)/shard_map/ppermute | solution.py:36
  48.2 2.0 %collective-permute-done.11.far = bf16[512,1024]{1,0:T(8,128)(2,1)S(1)} collective-permute-done((bf16[512,1024]{1,0:T(8,128)(2,1)S(1)}, bf16[512,1024]{1,0:T(8,128)(2,1)S(1)}, u32[]{:S(2)}, u32[]{:S(2)}) %collective-permute-start.11) | collective-permute-done | bytes 1048608 | tf_op jit(solution)/shard_map/ppermute | solution.py:36
  54.5 1.9 %collective-permute-start.13 = (bf16[128,1280]{1,0:T(8,128)(2,1)S(1)}, bf16[128,1280]{1,0:T(8,128)(2,1)S(1)}, u32[]{:S(2)}, u32[]{:S(2)}) collective-permute-start(bf16[128,1280]{1,0:T(8,128)(2,1)S(1)} %get-tuple-element.43), channel_id=1, source_target_pairs={{0,6},{2,4},{4,2},{6,0},{1,7},{3,5},{5,3},{7,1},{8,14},{10,12},{12... | collective-permute-start | bytes 983048 | tf_op jit(solution)/shard_map/ppermute | solution.py:36
  57.4 1.3 collective-permute-start.14
  58.8 2.0 %collective-permute-start.16 = (bf16[512,256]{1,0:T(8,128)(2,1)S(1)}, bf16[512,256]{1,0:T(8,128)(2,1)S(1)}, u32[]{:S(2)}, u32[]{:S(2)}) collective-permute-start(bf16[512,256]{1,0:T(8,128)(2,1)S(1)} %get-tuple-element.46), channel_id=1, source_target_pairs={{0,32},{16,48},{32,0},{48,16},{1,33},{17,49},{33,1},{49,17},{2,34}... | collective-permute-start | bytes 786440 | tf_op jit(solution)/shard_map/ppermute | solution.py:36
  60.8 9.9 %collective-permute-done.14.rx3 = bf16[512,256]{1,0:T(8,128)(2,1)S(1)} collective-permute-done((bf16[512,256]{1,0:T(8,128)(2,1)S(1)}, bf16[512,256]{1,0:T(8,128)(2,1)S(1)}, u32[]{:S(2)}, u32[]{:S(2)}) %collective-permute-start.14) | collective-permute-done | bytes 262176 | tf_op jit(solution)/shard_map/ppermute | solution.py:36
  71.3 1.2 ring_sum.1
  72.5 8.2 %all-to-all-start = ((bf16[8,96,512]{2,1,0:T(8,128)(2,1)}), bf16[8,96,512]{2,1,0:T(8,128)(2,1)S(1)}, u32[]{:S(2)}, u32[]{:S(2)}) async-start(bf16[8,96,512]{2,1,0:T(8,128)(2,1)} %bitcast.7), calls=%async_computation | async-start | bytes 1572864 | tf_op jit(solution)/shard_map/all_to_all | solution.py:496
  80.6 2.2 %collective-permute-start.19 = (bf16[8,64,512]{2,1,0:T(8,128)(2,1)S(1)}, bf16[8,64,512]{2,1,0:T(8,128)(2,1)S(1)}, u32[]{:S(2)}, u32[]{:S(2)}) collective-permute-start(bf16[8,64,512]{2,1,0:T(8,128)(2,1)S(1)} %pad_maximum_fusion.s0), channel_id=1, source_target_pairs={{0,4},{2,6},{4,0},{6,2},{1,5},{3,7},{5,1},{7,3},{8,12},{10,14},{12... | collective-permute-start | bytes 1572872 | tf_op jit(solution)/shard_map/ppermute | solution.py:36
  82.9 1.6 collective-permute-start.20
  84.5 18.2 %all-to-all-done.arrived = bf16[8,96,512]{2,1,0:T(8,128)(2,1)S(1)} async-done(((bf16[8,96,512]{2,1,0:T(8,128)(2,1)}), bf16[8,96,512]{2,1,0:T(8,128)(2,1)S(1)}, u32[]{:S(2)}, u32[]{:S(2)}) %all-to-all-start) | async-done | bytes 786464 | tf_op jit(solution)/shard_map/all_to_all | solution.py:496
  102.9 3.9 %collective-permute-start.28 = (bf16[32,512]{1,0:T(8,128)(2,1)S(1)}, bf16[32,512]{1,0:T(8,128)(2,1)S(1)}, u32[]{:S(2)}, u32[]{:S(2)}) collective-permute-start(bf16[32,512]{1,0:T(8,128)(2,1)S(1)} %slice.53), channel_id=1, source_target_pairs={{0,9},{1,8},{8,1},{9,0},{2,11},{3,10},{10,3},{11,2},{4,13},{5,12},... | collective-permute-start | bytes 98312 | tf_op jit(solution)/shard_map/ppermute | solution.py:503
  107.0 2.3 %collective-permute-start.22 = (bf16[128,512]{1,0:T(8,128)(2,1)S(1)}, bf16[128,512]{1,0:T(8,128)(2,1)S(1)}, u32[]{:S(2)}, u32[]{:S(2)}) collective-permute-start(bf16[128,512]{1,0:T(8,128)(2,1)S(1)} %pad_maximum_fusion.2.r0), channel_id=1, source_target_pairs={{0,4},{2,6},{4,0},{6,2},{1,5},{3,7},{5,1},{7,3},{8,12},{10,14},{12... | collective-permute-start | bytes 393224 | tf_op jit(solution)/shard_map/ppermute | solution.py:36
  109.2 1.6 collective-permute-start.23
  110.9 1.6 collective-permute-start.29
  112.4 1.1 collective-permute-start.30
  113.6 1.4 collective-permute-start.31
  115.6 3.9 %roots.2 = (bf16[64,512]{1,0:T(8,128)(2,1)S(1)}, f32[64,512]{1,0:T(8,128)S(1)}, f32[64,512]{1,0:T(8,128)S(1)}) custom-call(s32[41]{0:T(128)S(1)} %concatenate.28.place, bf16[128,512]{1,0:T(8,128)(2,1)S(1)} %pad_maximum_fusion.2.r0, bf16[128,512]{1,0:T(8,128)(2,1)S(1)} %collective-permute-done.21.r1, bf16[128,512]{1,0:T(8,128)(2,1)S(1)} %collective-permute-done.22.r2, ...), custom_call_target="tpu_custom_call" | custom-call | tf_op jit(solution)/shard_map/roots/pallas_call | solution.py:402
  120.6 2.0 %collective-permute-start.25 = (bf16[64,512]{1,0:T(8,128)(2,1)S(1)}, bf16[64,512]{1,0:T(8,128)(2,1)S(1)}, u32[]{:S(2)}, u32[]{:S(2)}) collective-permute-start(bf16[64,512]{1,0:T(8,128)(2,1)S(1)} %get-tuple-element.56), channel_id=1, source_target_pairs={{0,128},{64,192},{128,0},{192,64},{1,129},{65,193},{129,1},{193,65... | collective-permute-start | bytes 196616 | tf_op jit(solution)/shard_map/ppermute | solution.py:36
  122.7 2.6 %collective-permute-start.24 = (bf16[64,512]{1,0:T(8,128)(2,1)S(1)}, bf16[64,512]{1,0:T(8,128)(2,1)S(1)}, u32[]{:S(2)}, u32[]{:S(2)}) collective-permute-start(bf16[64,512]{1,0:T(8,128)(2,1)S(1)} %get-tuple-element.56), channel_id=1, source_target_pairs={{0,64},{64,0},{128,192},{192,128},{1,65},{65,1},{129,193},{193,129... | collective-permute-start | bytes 196616 | tf_op jit(solution)/shard_map/ppermute | solution.py:36
  126.2 2.7 %collective-permute-start.33 = (bf16[128,512]{1,0:T(8,128)(2,1)S(1)}, bf16[128,512]{1,0:T(8,128)(2,1)S(1)}, u32[]{:S(2)}, u32[]{:S(2)}) collective-permute-start(bf16[128,512]{1,0:T(8,128)(2,1)S(1)} %choose.1.r0), channel_id=1, source_target_pairs={{0,4},{2,6},{4,0},{6,2},{1,5},{3,7},{5,1},{7,3},{8,12},{10,14},{12... | collective-permute-start | bytes 393224 | tf_op jit(solution)/shard_map/ppermute | solution.py:36
  130.1 2.6 %collective-permute-done.33.r2 = bf16[128,512]{1,0:T(8,128)(2,1)S(1)} collective-permute-done((bf16[128,512]{1,0:T(8,128)(2,1)S(1)}, bf16[128,512]{1,0:T(8,128)(2,1)S(1)}, u32[]{:S(2)}, u32[]{:S(2)}) %collective-permute-start.33) | collective-permute-done | bytes 131104 | tf_op jit(solution)/shard_map/ppermute | solution.py:36
  132.7 1.4 collective-permute-done.34.r3
  134.4 1.3 collective-permute-start.36
  135.7 4.5 %roots.3 = (bf16[64,512]{1,0:T(8,128)(2,1)S(1)}, f32[2,64,512]{2,1,0:T(8,128)}, f32[2,64,512]{2,1,0:T(8,128)}) custom-call(s32[41]{0:T(128)S(1)} %concatenate.28.place, bf16[128,512]{1,0:T(8,128)(2,1)S(1)} %choose.1.r0, bf16[128,512]{1,0:T(8,128)(2,1)S(1)} %collective-permute-done.32.r1, bf16[128,512]{1,0:T(8,128)(2,1)S(1)} %collective-permute-done.33.r2, ...), custom_call_target="tpu_custom_call" | custom-call | tf_op jit(solution)/shard_map/roots/pallas_call | solution.py:402
  140.5 3.1 %collective-permute-start.38 = (bf16[64,512]{1,0:T(8,128)(2,1)S(1)}, bf16[64,512]{1,0:T(8,128)(2,1)S(1)}, u32[]{:S(2)}, u32[]{:S(2)}) collective-permute-start(bf16[64,512]{1,0:T(8,128)(2,1)S(1)} %get-tuple-element.64), channel_id=1, source_target_pairs={{0,128},{64,192},{128,0},{192,64},{1,129},{65,193},{129,1},{193,65... | collective-permute-start | bytes 196616 | tf_op jit(solution)/shard_map/ppermute | solution.py:36
  143.6 2.2 %collective-permute-start.39 = (bf16[64,512]{1,0:T(8,128)(2,1)S(1)}, bf16[64,512]{1,0:T(8,128)(2,1)S(1)}, u32[]{:S(2)}, u32[]{:S(2)}) collective-permute-start(bf16[64,512]{1,0:T(8,128)(2,1)S(1)} %get-tuple-element.64), channel_id=1, source_target_pairs={{0,192},{64,128},{128,64},{192,0},{1,193},{65,129},{129,65},{193,1... | collective-permute-start | bytes 196616 | tf_op jit(solution)/shard_map/ppermute | solution.py:36
  146.0 1.7 collective-permute-done.38
  147.7 1.3 collective-permute-done.39
  149.0 13.4 %collective-permute-start.44 = (bf16[1024,512]{1,0:T(8,128)(2,1)S(1)}, bf16[1024,512]{1,0:T(8,128)(2,1)S(1)}, u32[]{:S(2)}, u32[]{:S(2)}) collective-permute-start(bf16[1024,512]{1,0:T(8,128)(2,1)S(1)} %get-tuple-element.68.refs_0_), channel_id=1, source_target_pairs={{0,8},{8,0},{1,9},{9,1},{2,10},{10,2},{3,11},{11,3},{4,12},{12,4},... | collective-permute-start | bytes 3145736 | tf_op jit(solution)/shard_map/ppermute | solution.py:36
  163.4 1.4 collective-permute-start.41
  164.8 8.5 %collective-permute-done.40.refs_1_ = bf16[384,512]{1,0:T(8,128)(2,1)S(1)} collective-permute-done((bf16[384,512]{1,0:T(8,128)(2,1)S(1)}, bf16[384,512]{1,0:T(8,128)(2,1)S(1)}, u32[]{:S(2)}, u32[]{:S(2)}) %collective-permute-start.40) | collective-permute-done | bytes 393248 | tf_op jit(solution)/shard_map/ppermute | solution.py:36
  176.2 1.4 collective-permute-start.42
  177.7 4.9 %collective-permute-done.42.refs_3_ = bf16[128,512]{1,0:T(8,128)(2,1)S(1)} collective-permute-done((bf16[128,512]{1,0:T(8,128)(2,1)S(1)}, bf16[128,512]{1,0:T(8,128)(2,1)S(1)}, u32[]{:S(2)}, u32[]{:S(2)}) %collective-permute-start.42) | collective-permute-done | bytes 131104 | tf_op jit(solution)/shard_map/ppermute | solution.py:36
  184.8 2.0 %put_blocks.1 = bf16[64,18432]{1,0:T(8,128)(2,1)} custom-call(s32[41]{0:T(128)S(1)} %concatenate.28.place, bf16[1024,512]{1,0:T(8,128)(2,1)S(1)} %get-tuple-element.68.refs_0_, bf16[384,512]{1,0:T(8,128)(2,1)S(1)} %collective-permute-done.40.refs_1_, bf16[384,512]{1,0:T(8,128)(2,1)S(1)} %collective-permute-done.41.refs_2_, ...), custom_call_target="tpu_custom_call" | custom-call | tf_op jit(solution)/shard_map/put_blocks/pallas_call | solution.py:453
  (102 shorter events, 21.8 us)
Async XLA Ops:
  4.5 25.1 %collective-permute-start = (bf16[128,4352]{1,0:T(8,128)(2,1)S(1)}, bf16[128,4352]{1,0:T(8,128)(2,1)S(1)}, u32[]{:S(2)}, u32[]{:S(2)}) collective-permute-start(bf16[128,4352]{1,0:T(8,128)(2,1)S(1)} %get-tuple-element.35), channel_id=1, source_target_pairs={{0,16},{16,0},{32,48},{48,32},{1,17},{17,1},{33,49},{49,33},{2,18}... | collective-permute-start | bytes 3342344 | tf_op jit(solution)/shard_map/ppermute | solution.py:36
  6.6 26.8 %collective-permute-start.1 = (bf16[128,4352]{1,0:T(8,128)(2,1)S(1)}, bf16[128,4352]{1,0:T(8,128)(2,1)S(1)}, u32[]{:S(2)}, u32[]{:S(2)}) collective-permute-start(bf16[128,4352]{1,0:T(8,128)(2,1)S(1)} %get-tuple-element.36), channel_id=1, source_target_pairs={{0,48},{16,32},{32,16},{48,0},{1,49},{17,33},{33,17},{49,1},{2,50}... | collective-permute-start | bytes 3342344 | tf_op jit(solution)/shard_map/ppermute | solution.py:36
  10.4 23.2 %collective-permute-start.6 = (bf16[128,3584]{1,0:T(8,128)(2,1)S(1)}, bf16[128,3584]{1,0:T(8,128)(2,1)S(1)}, u32[]{:S(2)}, u32[]{:S(2)}) collective-permute-start(bf16[128,3584]{1,0:T(8,128)(2,1)S(1)} %get-tuple-element.38), channel_id=1, source_target_pairs={{0,2},{2,0},{4,6},{6,4},{1,3},{3,1},{5,7},{7,5},{8,10},{10,8},{12,... | collective-permute-start | bytes 2752520 | tf_op jit(solution)/shard_map/ppermute | solution.py:36
  11.8 21.9 %collective-permute-start.7 = (bf16[128,3584]{1,0:T(8,128)(2,1)S(1)}, bf16[128,3584]{1,0:T(8,128)(2,1)S(1)}, u32[]{:S(2)}, u32[]{:S(2)}) collective-permute-start(bf16[128,3584]{1,0:T(8,128)(2,1)S(1)} %get-tuple-element.39), channel_id=1, source_target_pairs={{0,6},{2,4},{4,2},{6,0},{1,7},{3,5},{5,3},{7,1},{8,14},{10,12},{12... | collective-permute-start | bytes 2752520 | tf_op jit(solution)/shard_map/ppermute | solution.py:36
  13.7 19.8 %collective-permute-start.8 = (bf16[4,64,512]{2,1,0:T(8,128)(2,1)S(1)}, bf16[4,64,512]{2,1,0:T(8,128)(2,1)S(1)}, u32[]{:S(2)}, u32[]{:S(2)}) collective-permute-start(bf16[4,64,512]{2,1,0:T(8,128)(2,1)S(1)} %cast_rows.1), channel_id=1, source_target_pairs={{0,1},{1,0},{2,3},{3,2},{4,5},{5,4},{6,7},{7,6},{8,9},{9,8},{10,11... | collective-permute-start | bytes 786440 | tf_op jit(solution)/shard_map/ppermute | solution.py:36
  29.6 11.5 %collective-permute-start.2 = (bf16[128,1536]{1,0:T(8,128)(2,1)S(1)}, bf16[128,1536]{1,0:T(8,128)(2,1)S(1)}, u32[]{:S(2)}, u32[]{:S(2)}) collective-permute-start(bf16[128,1536]{1,0:T(8,128)(2,1)S(1)} %slice.48), channel_id=1, source_target_pairs={{0,48},{16,32},{32,16},{48,0},{1,49},{17,33},{33,17},{49,1},{2,50}... | collective-permute-start | bytes 1179656 | tf_op jit(solution)/shard_map/ppermute | solution.py:36
  33.5 8.9 %collective-permute-start.3 = (bf16[128,1536]{1,0:T(8,128)(2,1)S(1)}, bf16[128,1536]{1,0:T(8,128)(2,1)S(1)}, u32[]{:S(2)}, u32[]{:S(2)}) collective-permute-start(bf16[128,1536]{1,0:T(8,128)(2,1)S(1)} %slice.49), channel_id=1, source_target_pairs={{0,16},{16,0},{32,48},{48,32},{1,17},{17,1},{33,49},{49,33},{2,18}... | collective-permute-start | bytes 1179656 | tf_op jit(solution)/shard_map/ppermute | solution.py:36
  33.7 12.4 %collective-permute-start.9 = (bf16[128,1280]{1,0:T(8,128)(2,1)S(1)}, bf16[128,1280]{1,0:T(8,128)(2,1)S(1)}, u32[]{:S(2)}, u32[]{:S(2)}) collective-permute-start(bf16[128,1280]{1,0:T(8,128)(2,1)S(1)} %slice.50), channel_id=1, source_target_pairs={{0,6},{2,4},{4,2},{6,0},{1,7},{3,5},{5,3},{7,1},{8,14},{10,12},{12... | collective-permute-start | bytes 983048 | tf_op jit(solution)/shard_map/ppermute | solution.py:36
  36.5 9.6 %collective-permute-start.10 = (bf16[128,1280]{1,0:T(8,128)(2,1)S(1)}, bf16[128,1280]{1,0:T(8,128)(2,1)S(1)}, u32[]{:S(2)}, u32[]{:S(2)}) collective-permute-start(bf16[128,1280]{1,0:T(8,128)(2,1)S(1)} %slice.51), channel_id=1, source_target_pairs={{0,2},{2,0},{4,6},{6,4},{1,3},{3,1},{5,7},{7,5},{8,10},{10,8},{12,... | collective-permute-start | bytes 983048 | tf_op jit(solution)/shard_map/ppermute | solution.py:36
  43.2 9.9 %collective-permute-start.4 = (bf16[512,1280]{1,0:T(8,128)(2,1)S(1)}, bf16[512,1280]{1,0:T(8,128)(2,1)S(1)}, u32[]{:S(2)}, u32[]{:S(2)}) collective-permute-start(bf16[512,1280]{1,0:T(8,128)(2,1)S(1)} %partials.5), channel_id=1, source_target_pairs={{0,8},{8,0},{1,9},{9,1},{2,10},{10,2},{3,11},{11,3},{4,12},{12,4},... | collective-permute-start | bytes 3932168 | tf_op jit(solution)/shard_map/ppermute | solution.py:36
  46.8 3.4 %collective-permute-start.11 = (bf16[512,1024]{1,0:T(8,128)(2,1)S(1)}, bf16[512,1024]{1,0:T(8,128)(2,1)S(1)}, u32[]{:S(2)}, u32[]{:S(2)}) collective-permute-start(bf16[512,1024]{1,0:T(8,128)(2,1)S(1)} %partials.7), channel_id=1, source_target_pairs={{0,8},{8,0},{1,9},{9,1},{2,10},{10,2},{3,11},{11,3},{4,12},{12,4},... | collective-permute-start | bytes 3145736 | tf_op jit(solution)/shard_map/ppermute | solution.py:36
  51.2 7.6 %collective-permute-start.12 = (bf16[512,256]{1,0:T(8,128)(2,1)S(1)}, bf16[512,256]{1,0:T(8,128)(2,1)S(1)}, u32[]{:S(2)}, u32[]{:S(2)}) collective-permute-start(bf16[512,256]{1,0:T(8,128)(2,1)S(1)} %get-tuple-element.42), channel_id=1, source_target_pairs={{0,16},{16,0},{32,48},{48,32},{1,17},{17,1},{33,49},{49,33},{2,18}... | collective-permute-start | bytes 786440 | tf_op jit(solution)/shard_map/ppermute | solution.py:36
  54.0 16.7 %collective-permute-start.5 = (bf16[128,1280]{1,0:T(8,128)(2,1)S(1)}, bf16[128,1280]{1,0:T(8,128)(2,1)S(1)}, u32[]{:S(2)}, u32[]{:S(2)}) collective-permute-start(bf16[128,1280]{1,0:T(8,128)(2,1)S(1)} %get-tuple-element.37), channel_id=1, source_target_pairs={{0,2},{2,0},{4,6},{6,4},{1,3},{3,1},{5,7},{7,5},{8,10},{10,8},{12,... | collective-permute-start | bytes 983048 | tf_op jit(solution)/shard_map/ppermute | solution.py:36
  54.5 16.2 %collective-permute-start.13 = (bf16[128,1280]{1,0:T(8,128)(2,1)S(1)}, bf16[128,1280]{1,0:T(8,128)(2,1)S(1)}, u32[]{:S(2)}, u32[]{:S(2)}) collective-permute-start(bf16[128,1280]{1,0:T(8,128)(2,1)S(1)} %get-tuple-element.43), channel_id=1, source_target_pairs={{0,6},{2,4},{4,2},{6,0},{1,7},{3,5},{5,3},{7,1},{8,14},{10,12},{12... | collective-permute-start | bytes 983048 | tf_op jit(solution)/shard_map/ppermute | solution.py:36
  56.4 14.9 %collective-permute-start.15 = (bf16[128,1280]{1,0:T(8,128)(2,1)S(1)}, bf16[128,1280]{1,0:T(8,128)(2,1)S(1)}, u32[]{:S(2)}, u32[]{:S(2)}) collective-permute-start(bf16[128,1280]{1,0:T(8,128)(2,1)S(1)} %get-tuple-element.45), channel_id=1, source_target_pairs={{0,4},{2,6},{4,0},{6,2},{1,5},{3,7},{5,1},{7,3},{8,12},{10,14},{12... | collective-permute-start | bytes 983048 | tf_op jit(solution)/shard_map/ppermute | solution.py:36
  57.4 13.3 %collective-permute-start.14 = (bf16[512,256]{1,0:T(8,128)(2,1)S(1)}, bf16[512,256]{1,0:T(8,128)(2,1)S(1)}, u32[]{:S(2)}, u32[]{:S(2)}) collective-permute-start(bf16[512,256]{1,0:T(8,128)(2,1)S(1)} %get-tuple-element.44), channel_id=1, source_target_pairs={{0,48},{16,32},{32,16},{48,0},{1,49},{17,33},{33,17},{49,1},{2,50}... | collective-permute-start | bytes 786440 | tf_op jit(solution)/shard_map/ppermute | solution.py:36
  58.8 11.9 %collective-permute-start.16 = (bf16[512,256]{1,0:T(8,128)(2,1)S(1)}, bf16[512,256]{1,0:T(8,128)(2,1)S(1)}, u32[]{:S(2)}, u32[]{:S(2)}) collective-permute-start(bf16[512,256]{1,0:T(8,128)(2,1)S(1)} %get-tuple-element.46), channel_id=1, source_target_pairs={{0,32},{16,48},{32,0},{48,16},{1,33},{17,49},{33,1},{49,17},{2,34}... | collective-permute-start | bytes 786440 | tf_op jit(solution)/shard_map/ppermute | solution.py:36
  72.5 30.2 %all-to-all-start = ((bf16[8,96,512]{2,1,0:T(8,128)(2,1)}), bf16[8,96,512]{2,1,0:T(8,128)(2,1)S(1)}, u32[]{:S(2)}, u32[]{:S(2)}) async-start(bf16[8,96,512]{2,1,0:T(8,128)(2,1)} %bitcast.7), calls=%async_computation | async-start | bytes 1572864 | tf_op jit(solution)/shard_map/all_to_all | solution.py:496
  80.6 26.2 %collective-permute-start.18 = (bf16[8,64,512]{2,1,0:T(8,128)(2,1)S(1)}, bf16[8,64,512]{2,1,0:T(8,128)(2,1)S(1)}, u32[]{:S(2)}, u32[]{:S(2)}) collective-permute-start(bf16[8,64,512]{2,1,0:T(8,128)(2,1)S(1)} %pad_maximum_fusion.s0), channel_id=1, source_target_pairs={{0,2},{2,0},{4,6},{6,4},{1,3},{3,1},{5,7},{7,5},{8,10},{10,8},{12,... | collective-permute-start | bytes 1572872 | tf_op jit(solution)/shard_map/ppermute | solution.py:36
  80.6 26.2 %collective-permute-start.19 = (bf16[8,64,512]{2,1,0:T(8,128)(2,1)S(1)}, bf16[8,64,512]{2,1,0:T(8,128)(2,1)S(1)}, u32[]{:S(2)}, u32[]{:S(2)}) collective-permute-start(bf16[8,64,512]{2,1,0:T(8,128)(2,1)S(1)} %pad_maximum_fusion.s0), channel_id=1, source_target_pairs={{0,4},{2,6},{4,0},{6,2},{1,5},{3,7},{5,1},{7,3},{8,12},{10,14},{12... | collective-permute-start | bytes 1572872 | tf_op jit(solution)/shard_map/ppermute | solution.py:36
  82.9 23.9 %collective-permute-start.20 = (bf16[8,64,512]{2,1,0:T(8,128)(2,1)S(1)}, bf16[8,64,512]{2,1,0:T(8,128)(2,1)S(1)}, u32[]{:S(2)}, u32[]{:S(2)}) collective-permute-start(bf16[8,64,512]{2,1,0:T(8,128)(2,1)S(1)} %pad_maximum_fusion.s0), channel_id=1, source_target_pairs={{0,6},{2,4},{4,2},{6,0},{1,7},{3,5},{5,3},{7,1},{8,14},{10,12},{12... | collective-permute-start | bytes 1572872 | tf_op jit(solution)/shard_map/ppermute | solution.py:36
  102.8 4.0 %collective-permute-start.17 = (bf16[96,512]{1,0:T(8,128)(2,1)S(1)}, bf16[96,512]{1,0:T(8,128)(2,1)S(1)}, u32[]{:S(2)}, u32[]{:S(2)}) collective-permute-start(bf16[96,512]{1,0:T(8,128)(2,1)S(1)} %line_sum.1), channel_id=1, source_target_pairs={{0,1},{1,0},{2,3},{3,2},{4,5},{5,4},{6,7},{7,6},{8,9},{9,8},{10,11... | collective-permute-start | bytes 294920 | tf_op jit(solution)/shard_map/ppermute | solution.py:36
  102.9 7.9 %collective-permute-start.28 = (bf16[32,512]{1,0:T(8,128)(2,1)S(1)}, bf16[32,512]{1,0:T(8,128)(2,1)S(1)}, u32[]{:S(2)}, u32[]{:S(2)}) collective-permute-start(bf16[32,512]{1,0:T(8,128)(2,1)S(1)} %slice.53), channel_id=1, source_target_pairs={{0,9},{1,8},{8,1},{9,0},{2,11},{3,10},{10,3},{11,2},{4,13},{5,12},... | collective-permute-start | bytes 98312 | tf_op jit(solution)/shard_map/ppermute | solution.py:503
  106.8 4.0 %collective-permute-start.27 = (bf16[32,512]{1,0:T(8,128)(2,1)S(1)}, bf16[32,512]{1,0:T(8,128)(2,1)S(1)}, u32[]{:S(2)}, u32[]{:S(2)}) collective-permute-start(bf16[32,512]{1,0:T(8,128)(2,1)S(1)} %slice.53), channel_id=1, source_target_pairs={{0,8},{8,0},{1,9},{9,1},{2,10},{10,2},{3,11},{11,3},{4,12},{12,4},... | collective-permute-start | bytes 98312 | tf_op jit(solution)/shard_map/ppermute | solution.py:36
  106.9 6.7 %collective-permute-start.21 = (bf16[128,512]{1,0:T(8,128)(2,1)S(1)}, bf16[128,512]{1,0:T(8,128)(2,1)S(1)}, u32[]{:S(2)}, u32[]{:S(2)}) collective-permute-start(bf16[128,512]{1,0:T(8,128)(2,1)S(1)} %pad_maximum_fusion.2.r0), channel_id=1, source_target_pairs={{0,2},{2,0},{4,6},{6,4},{1,3},{3,1},{5,7},{7,5},{8,10},{10,8},{12,... | collective-permute-start | bytes 393224 | tf_op jit(solution)/shard_map/ppermute | solution.py:36
  107.0 8.6 %collective-permute-start.22 = (bf16[128,512]{1,0:T(8,128)(2,1)S(1)}, bf16[128,512]{1,0:T(8,128)(2,1)S(1)}, u32[]{:S(2)}, u32[]{:S(2)}) collective-permute-start(bf16[128,512]{1,0:T(8,128)(2,1)S(1)} %pad_maximum_fusion.2.r0), channel_id=1, source_target_pairs={{0,4},{2,6},{4,0},{6,2},{1,5},{3,7},{5,1},{7,3},{8,12},{10,14},{12... | collective-permute-start | bytes 393224 | tf_op jit(solution)/shard_map/ppermute | solution.py:36
  109.2 6.4 %collective-permute-start.23 = (bf16[128,512]{1,0:T(8,128)(2,1)S(1)}, bf16[128,512]{1,0:T(8,128)(2,1)S(1)}, u32[]{:S(2)}, u32[]{:S(2)}) collective-permute-start(bf16[128,512]{1,0:T(8,128)(2,1)S(1)} %pad_maximum_fusion.2.r0), channel_id=1, source_target_pairs={{0,6},{2,4},{4,2},{6,0},{1,7},{3,5},{5,3},{7,1},{8,14},{10,12},{12... | collective-permute-start | bytes 393224 | tf_op jit(solution)/shard_map/ppermute | solution.py:36
  110.9 11.8 %collective-permute-start.29 = (bf16[128,512]{1,0:T(8,128)(2,1)S(1)}, bf16[128,512]{1,0:T(8,128)(2,1)S(1)}, u32[]{:S(2)}, u32[]{:S(2)}) collective-permute-start(bf16[128,512]{1,0:T(8,128)(2,1)S(1)} %pad_maximum_fusion.3.q0), channel_id=1, source_target_pairs={{0,16},{16,0},{32,48},{48,32},{1,17},{17,1},{33,49},{49,33},{2,18}... | collective-permute-start | bytes 393224 | tf_op jit(solution)/shard_map/ppermute | solution.py:36
  112.4 12.8 %collective-permute-start.30 = (bf16[128,512]{1,0:T(8,128)(2,1)S(1)}, bf16[128,512]{1,0:T(8,128)(2,1)S(1)}, u32[]{:S(2)}, u32[]{:S(2)}) collective-permute-start(bf16[128,512]{1,0:T(8,128)(2,1)S(1)} %pad_maximum_fusion.3.q0), channel_id=1, source_target_pairs={{0,32},{16,48},{32,0},{48,16},{1,33},{17,49},{33,1},{49,17},{2,34}... | collective-permute-start | bytes 393224 | tf_op jit(solution)/shard_map/ppermute | solution.py:36
  113.6 11.7 %collective-permute-start.31 = (bf16[128,512]{1,0:T(8,128)(2,1)S(1)}, bf16[128,512]{1,0:T(8,128)(2,1)S(1)}, u32[]{:S(2)}, u32[]{:S(2)}) collective-permute-start(bf16[128,512]{1,0:T(8,128)(2,1)S(1)} %pad_maximum_fusion.3.q0), channel_id=1, source_target_pairs={{0,48},{16,32},{32,16},{48,0},{1,49},{17,33},{33,17},{49,1},{2,50}... | collective-permute-start | bytes 393224 | tf_op jit(solution)/shard_map/ppermute | solution.py:36
  119.5 9.4 %collective-permute-start.26 = (bf16[64,512]{1,0:T(8,128)(2,1)S(1)}, bf16[64,512]{1,0:T(8,128)(2,1)S(1)}, u32[]{:S(2)}, u32[]{:S(2)}) collective-permute-start(bf16[64,512]{1,0:T(8,128)(2,1)S(1)} %get-tuple-element.56), channel_id=1, source_target_pairs={{0,192},{64,128},{128,64},{192,0},{1,193},{65,129},{129,65},{193,1... | collective-permute-start | bytes 196616 | tf_op jit(solution)/shard_map/ppermute | solution.py:36
  120.6 9.4 %collective-permute-start.25 = (bf16[64,512]{1,0:T(8,128)(2,1)S(1)}, bf16[64,512]{1,0:T(8,128)(2,1)S(1)}, u32[]{:S(2)}, u32[]{:S(2)}) collective-permute-start(bf16[64,512]{1,0:T(8,128)(2,1)S(1)} %get-tuple-element.56), channel_id=1, source_target_pairs={{0,128},{64,192},{128,0},{192,64},{1,129},{65,193},{129,1},{193,65... | collective-permute-start | bytes 196616 | tf_op jit(solution)/shard_map/ppermute | solution.py:36
  122.7 7.4 %collective-permute-start.24 = (bf16[64,512]{1,0:T(8,128)(2,1)S(1)}, bf16[64,512]{1,0:T(8,128)(2,1)S(1)}, u32[]{:S(2)}, u32[]{:S(2)}) collective-permute-start(bf16[64,512]{1,0:T(8,128)(2,1)S(1)} %get-tuple-element.56), channel_id=1, source_target_pairs={{0,64},{64,0},{128,192},{192,128},{1,65},{65,1},{129,193},{193,129... | collective-permute-start | bytes 196616 | tf_op jit(solution)/shard_map/ppermute | solution.py:36
  125.9 4.2 %collective-permute-start.32 = (bf16[128,512]{1,0:T(8,128)(2,1)S(1)}, bf16[128,512]{1,0:T(8,128)(2,1)S(1)}, u32[]{:S(2)}, u32[]{:S(2)}) collective-permute-start(bf16[128,512]{1,0:T(8,128)(2,1)S(1)} %choose.1.r0), channel_id=1, source_target_pairs={{0,2},{2,0},{4,6},{6,4},{1,3},{3,1},{5,7},{7,5},{8,10},{10,8},{12,... | collective-permute-start | bytes 393224 | tf_op jit(solution)/shard_map/ppermute | solution.py:36
  126.2 6.5 %collective-permute-start.33 = (bf16[128,512]{1,0:T(8,128)(2,1)S(1)}, bf16[128,512]{1,0:T(8,128)(2,1)S(1)}, u32[]{:S(2)}, u32[]{:S(2)}) collective-permute-start(bf16[128,512]{1,0:T(8,128)(2,1)S(1)} %choose.1.r0), channel_id=1, source_target_pairs={{0,4},{2,6},{4,0},{6,2},{1,5},{3,7},{5,1},{7,3},{8,12},{10,14},{12... | collective-permute-start | bytes 393224 | tf_op jit(solution)/shard_map/ppermute | solution.py:36
  128.9 5.2 %collective-permute-start.34 = (bf16[128,512]{1,0:T(8,128)(2,1)S(1)}, bf16[128,512]{1,0:T(8,128)(2,1)S(1)}, u32[]{:S(2)}, u32[]{:S(2)}) collective-permute-start(bf16[128,512]{1,0:T(8,128)(2,1)S(1)} %choose.1.r0), channel_id=1, source_target_pairs={{0,6},{2,4},{4,2},{6,0},{1,7},{3,5},{5,3},{7,1},{8,14},{10,12},{12... | collective-permute-start | bytes 393224 | tf_op jit(solution)/shard_map/ppermute | solution.py:36
  134.1 11.8 %collective-permute-start.35 = (bf16[256,512]{1,0:T(8,128)(2,1)S(1)}, bf16[256,512]{1,0:T(8,128)(2,1)S(1)}, u32[]{:S(2)}, u32[]{:S(2)}) collective-permute-start(bf16[256,512]{1,0:T(8,128)(2,1)S(1)} %pad_maximum_fusion.1), channel_id=1, source_target_pairs={{0,16},{16,0},{32,48},{48,32},{1,17},{17,1},{33,49},{49,33},{2,18}... | collective-permute-start | bytes 786440 | tf_op jit(solution)/shard_map/ppermute | solution.py:36
  134.4 11.5 %collective-permute-start.36 = (bf16[256,512]{1,0:T(8,128)(2,1)S(1)}, bf16[256,512]{1,0:T(8,128)(2,1)S(1)}, u32[]{:S(2)}, u32[]{:S(2)}) collective-permute-start(bf16[256,512]{1,0:T(8,128)(2,1)S(1)} %pad_maximum_fusion.1), channel_id=1, source_target_pairs={{0,48},{16,32},{32,16},{48,0},{1,49},{17,33},{33,17},{49,1},{2,50}... | collective-permute-start | bytes 786440 | tf_op jit(solution)/shard_map/ppermute | solution.py:36
  140.2 5.8 %collective-permute-start.37 = (bf16[64,512]{1,0:T(8,128)(2,1)S(1)}, bf16[64,512]{1,0:T(8,128)(2,1)S(1)}, u32[]{:S(2)}, u32[]{:S(2)}) collective-permute-start(bf16[64,512]{1,0:T(8,128)(2,1)S(1)} %get-tuple-element.64), channel_id=1, source_target_pairs={{0,64},{64,0},{128,192},{192,128},{1,65},{65,1},{129,193},{193,129... | collective-permute-start | bytes 196616 | tf_op jit(solution)/shard_map/ppermute | solution.py:36
  140.5 7.2 %collective-permute-start.38 = (bf16[64,512]{1,0:T(8,128)(2,1)S(1)}, bf16[64,512]{1,0:T(8,128)(2,1)S(1)}, u32[]{:S(2)}, u32[]{:S(2)}) collective-permute-start(bf16[64,512]{1,0:T(8,128)(2,1)S(1)} %get-tuple-element.64), channel_id=1, source_target_pairs={{0,128},{64,192},{128,0},{192,64},{1,129},{65,193},{129,1},{193,65... | collective-permute-start | bytes 196616 | tf_op jit(solution)/shard_map/ppermute | solution.py:36
  143.6 5.4 %collective-permute-start.39 = (bf16[64,512]{1,0:T(8,128)(2,1)S(1)}, bf16[64,512]{1,0:T(8,128)(2,1)S(1)}, u32[]{:S(2)}, u32[]{:S(2)}) collective-permute-start(bf16[64,512]{1,0:T(8,128)(2,1)S(1)} %get-tuple-element.64), channel_id=1, source_target_pairs={{0,192},{64,128},{128,64},{192,0},{1,193},{65,129},{129,65},{193,1... | collective-permute-start | bytes 196616 | tf_op jit(solution)/shard_map/ppermute | solution.py:36
  149.0 35.7 %collective-permute-start.44 = (bf16[1024,512]{1,0:T(8,128)(2,1)S(1)}, bf16[1024,512]{1,0:T(8,128)(2,1)S(1)}, u32[]{:S(2)}, u32[]{:S(2)}) collective-permute-start(bf16[1024,512]{1,0:T(8,128)(2,1)S(1)} %get-tuple-element.68.refs_0_), channel_id=1, source_target_pairs={{0,8},{8,0},{1,9},{9,1},{2,10},{10,2},{3,11},{11,3},{4,12},{12,4},... | collective-permute-start | bytes 3145736 | tf_op jit(solution)/shard_map/ppermute | solution.py:36
  162.5 10.8 %collective-permute-start.40 = (bf16[384,512]{1,0:T(8,128)(2,1)S(1)}, bf16[384,512]{1,0:T(8,128)(2,1)S(1)}, u32[]{:S(2)}, u32[]{:S(2)}) collective-permute-start(bf16[384,512]{1,0:T(8,128)(2,1)S(1)} %slice_dynamic-update-slice_fusion.1), channel_id=1, source_target_pairs={{0,16},{16,0},{32,48},{48,32},{1,17},{17,1},{33,49},{49,33},{2,18}... | collective-permute-start | bytes 1179656 | tf_op jit(solution)/shard_map/ppermute | solution.py:36
  163.4 11.7 %collective-permute-start.41 = (bf16[384,512]{1,0:T(8,128)(2,1)S(1)}, bf16[384,512]{1,0:T(8,128)(2,1)S(1)}, u32[]{:S(2)}, u32[]{:S(2)}) collective-permute-start(bf16[384,512]{1,0:T(8,128)(2,1)S(1)} %slice_dynamic-update-slice_fusion), channel_id=1, source_target_pairs={{0,48},{16,32},{32,16},{48,0},{1,49},{17,33},{33,17},{49,1},{2,50}... | collective-permute-start | bytes 1179656 | tf_op jit(solution)/shard_map/ppermute | solution.py:36
  173.3 11.5 %collective-permute-start.45 = (bf16[384,512]{1,0:T(8,128)(2,1)S(1)}, bf16[384,512]{1,0:T(8,128)(2,1)S(1)}, u32[]{:S(2)}, u32[]{:S(2)}) collective-permute-start(bf16[384,512]{1,0:T(8,128)(2,1)S(1)} %collective-permute-done.40.refs_1_), channel_id=1, source_target_pairs={{0,8},{8,0},{1,9},{9,1},{2,10},{10,2},{3,11},{11,3},{4,12},{12,4},... | collective-permute-start | bytes 1179656 | tf_op jit(solution)/shard_map/ppermute | solution.py:36
  175.1 9.7 %collective-permute-start.46 = (bf16[384,512]{1,0:T(8,128)(2,1)S(1)}, bf16[384,512]{1,0:T(8,128)(2,1)S(1)}, u32[]{:S(2)}, u32[]{:S(2)}) collective-permute-start(bf16[384,512]{1,0:T(8,128)(2,1)S(1)} %collective-permute-done.41.refs_2_), channel_id=1, source_target_pairs={{0,8},{8,0},{1,9},{9,1},{2,10},{10,2},{3,11},{11,3},{4,12},{12,4},... | collective-permute-start | bytes 1179656 | tf_op jit(solution)/shard_map/ppermute | solution.py:36
  176.2 6.4 %collective-permute-start.42 = (bf16[128,512]{1,0:T(8,128)(2,1)S(1)}, bf16[128,512]{1,0:T(8,128)(2,1)S(1)}, u32[]{:S(2)}, u32[]{:S(2)}) collective-permute-start(bf16[128,512]{1,0:T(8,128)(2,1)S(1)} %slice.56), channel_id=1, source_target_pairs={{0,48},{16,32},{32,16},{48,0},{1,49},{17,33},{33,17},{49,1},{2,50}... | collective-permute-start | bytes 393224 | tf_op jit(solution)/shard_map/ppermute | solution.py:36
  177.6 5.8 %collective-permute-start.43 = (bf16[128,512]{1,0:T(8,128)(2,1)S(1)}, bf16[128,512]{1,0:T(8,128)(2,1)S(1)}, u32[]{:S(2)}, u32[]{:S(2)}) collective-permute-start(bf16[128,512]{1,0:T(8,128)(2,1)S(1)} %slice.57), channel_id=1, source_target_pairs={{0,16},{16,0},{32,48},{48,32},{1,17},{17,1},{33,49},{49,33},{2,18}... | collective-permute-start | bytes 393224 | tf_op jit(solution)/shard_map/ppermute | solution.py:36
  (6 other events, 26.8 us)
where the time goes:
time: 187 us
  starting transfers between devices  88.3 us (47%)
  waiting for transfers between devices  71.2 us (38%)
  Pallas kernels  24.1 us (13%)
  local copies, waits for them, and re-layouts  1.94 us (1%)
    ppermute x48, starting transfers between devices, swap(): return lax.ppermute(value, axis, [(i, i ^ mask) for i in range(size)])  76.3 us
    ppermute x48, waiting for transfers between devices, swap(): return lax.ppermute(value, axis, [(i, i ^ mask) for i in range(size)])  53 us
    all_to_all x1, waiting for transfers between devices, shards(): message = lax.all_to_all(message, ('z_hi', 'z_lo'), 0, 0, tiled=True)  18.2 us
    pallas_call x2, Pallas kernels, roots(): pl.pallas_call(functools.partial(root_kernel, slot), out_shape=[jax.Shape...  8.38 us
    all_to_all x1, starting transfers between devices, shards(): message = lax.all_to_all(message, ('z_hi', 'z_lo'), 0, 0, tiled=True)  8.18 us
    pallas_call x3, Pallas kernels, packed(): pl.pallas_call(kernel, out_shape=[jax.ShapeDtypeStruct((rows, w), jnp.bfl...  6.06 us
    ppermute x1, starting transfers between devices, shards(): extra_far = lax.ppermute(extra, ('core', 'z_lo'), diagonal)  3.88 us
  transfers between devices with their start and end apart: 50, of which 17 were waited for; matrix products, arithmetic and copies ran while one was open for 0% of the time, Pallas kernels for 10%

commit v1 on v0

--- a/solution.py
+++ b/solution.py
@@ -415,11 +415,11 @@
 
 
 def place_kernel(place, *refs):
-    sources, out, position, sem = refs[:10], refs[10], refs[11], refs[12]
+    sources, out, position, sem = refs[:8], refs[8], refs[9], refs[10]
     fill_positions(place, position)
     my_z, my_x, my_core = place[0], place[1], place[2]
 
-    def find(slot, r, a, held, near1, near3, low, high):
+    def find(slot, r, a, held, near1, near3, far):
         if r == 0:
             return held, slot * 3 * 4 + a
         if slot == 0 and r == 2:
@@ -427,7 +427,7 @@
         if slot == 0:
             return held, (1 if r == 1 else 2) * 4 + a
         if r == 2:
-            return (low, a) if a < 2 else (high, a - 2)
+            return far, a
         return (near1 if r == 1 else near3), a
 
     for wait in (False, True):
@@ -435,7 +435,7 @@
             for flip in range(2):
                 for r in range(4):
                     for a in range(4):
-                        source, row = find(slot, r, a, *sources[flip * 5 : flip * 5 + 5])
+                        source, row = find(slot, r, a, *sources[flip * 4 : flip * 4 + 4])
                         block = position[((my_z ^ a) * 4 + (my_x ^ r)) * 2 + (my_core ^ flip)]
                         copy = pltpu.make_async_copy(
                             source.at[pl.ds(row * 64, 64), :],
@@ -453,7 +453,7 @@
     return pl.pallas_call(
         place_kernel,
         out_shape=jax.ShapeDtypeStruct((64, blocks * B), jnp.bfloat16),
-        in_specs=[SMEM] + [ANY] * 10,
+        in_specs=[SMEM] + [ANY] * 8,
         out_specs=ANY,
         scratch_shapes=[pltpu.SMEM((32,), jnp.int32), pltpu.SemaphoreType.DMA],
         compiler_params=PARAMS,
@@ -501,26 +501,28 @@
     extra_core = swap(extra, "core", 1)
     diagonal = [(c * 2 + w, 3 - (c * 2 + w)) for c in range(2) for w in range(2)]
     extra_far = lax.ppermute(extra, ("core", "z_lo"), diagonal)
-    far, s1, s2, s3 = lax.optimization_barrier((far, s1, s2, s3))
+    m0 = jnp.concatenate([main, far[:64]])
+    m0, s1, s2, s3 = lax.optimization_barrier((m0, s1, s2, s3))
     statistics = whole(place, (statistics, s1, s2, s3))
-    m0 = jnp.concatenate([main, far[:64]])
     m2, m1, m3 = swap(m0, "y", 2), swap(m0, "y", 1), swap(m0, "y", 3)
     q0 = jnp.concatenate([extra, far[64:], extra_core, extra_far])
     q2, q1, q3 = swap(q0, "x", 2), swap(q0, "x", 1), swap(q0, "x", 3)
     first, left_first, right_first = roots(0, place, (m0, m1, m2, m3), statistics, stat_left[0], stat_right[0])
     e0 = choose(place, (q0, q1, q2, q3))
     e2, e1, e3 = swap(e0, "y", 2), swap(e0, "y", 1), swap(e0, "y", 3)
-    plane, e1, e2, e3 = lax.optimization_barrier((around_z(first), e1, e2, e3))
+    first, e1, e2, e3 = lax.optimization_barrier((first, e1, e2, e3))
+    plane = around_z(first)
     second, left_new, right_new = roots(
         1, place, (e0, e1, e2, e3), statistics, stat_left[0], stat_right[0], left_first, right_first
     )
-    _, second = lax.optimization_barrier((plane, second))
+    plane, second = lax.optimization_barrier((plane, second))
     first1, first3 = swap(plane, "x", 1), swap(plane, "x", 3)
     second = around_z(second)
+    far = swap(second, "x", 2)
     near1 = swap(jnp.concatenate([second, first3[128:]]), "x", 1)
     near3 = swap(jnp.concatenate([second, first1[:128]]), "x", 3)
     held = jnp.concatenate([plane, first1, first3, second])
-    sources = (held, near1, near3, swap(near1[:128], "x", 3), swap(near3[128:256], "x", 1))
+    sources = (held, near1, near3, far)
     out = put_blocks(place, sources + tuple(swap(v, "core", 1) for v in sources), bucket)
     return (out, left_new[None], right_new[None])
 

time: 187 us -> 183 us (0.979)
  starting transfers between devices: 88.3 us -> 78.4 us
  waiting for transfers between devices: 71.2 us -> 77.1 us
    ppermute x48 -> x46, starting transfers between devices: 76.3 us -> 66.4 us  [swap(): return lax.ppermute(value, axis, [(i, i ^ mask) for i in range(size)])]
    ppermute x48 -> x46, waiting for transfers between devices: 53 us -> 58.9 us  [swap(): return lax.ppermute(value, axis, [(i, i ^ mask) for i in range(size)])]
  transfers between devices with their start and end apart: 50 -> 48, of which waited for: 17 -> 21; matrix products, arithmetic and copies ran while one was open for 0% -> 0% of each run, Pallas kernels for 10% -> 10%
where the time goes in v1:
time: 183 us
  starting transfers between devices  78.4 us (43%)
  waiting for transfers between devices  77.1 us (42%)
  Pallas kernels  24.1 us (13%)
  local copies, waits for them, and re-layouts  1.91 us (1%)
    ppermute x46, starting transfers between devices, swap(): return lax.ppermute(value, axis, [(i, i ^ mask) for i in range(size)])  66.4 us
    ppermute x46, waiting for transfers between devices, swap(): return lax.ppermute(value, axis, [(i, i ^ mask) for i in range(size)])  58.9 us
    all_to_all x1, waiting for transfers between devices, shards(): message = lax.all_to_all(message, ('z_hi', 'z_lo'), 0, 0, tiled=True)  18.2 us
    pallas_call x2, Pallas kernels, roots(): pl.pallas_call(functools.partial(root_kernel, slot), out_shape=[jax.Shape...  8.39 us
    all_to_all x1, starting transfers between devices, shards(): message = lax.all_to_all(message, ('z_hi', 'z_lo'), 0, 0, tiled=True)  8.18 us
    pallas_call x3, Pallas kernels, packed(): pl.pallas_call(kernel, out_shape=[jax.ShapeDtypeStruct((rows, w), jnp.bfl...  6.06 us
    ppermute x1, starting transfers between devices, shards(): extra_far = lax.ppermute(extra, ('core', 'z_lo'), diagonal)  3.8 us
  transfers between devices with their start and end apart: 48, of which 21 were waited for; matrix products, arithmetic and copies ran while one was open for 0% of the time, Pallas kernels for 10%

profile of v1, /device:TPU:1, one launch (start us, length us, event | category | flops | bytes accessed | tf_op | source)
XLA Modules:
  0.0 182.9 jit_solution(11575613756960352063)
XLA Ops:
  2.3 2.2 %pack_x.1 = (bf16[128,4352]{1,0:T(8,128)(2,1)S(1)}, bf16[128,4352]{1,0:T(8,128)(2,1)S(1)}) custom-call(s32[41]{0:T(128)S(1)} %concatenate.30.place, bf16[128,18432]{1,0:T(8,128)(2,1)} %d.5, bf16[128,512]{1,0:T(8,128)(2,1)S(1)} %copy-done), custom_call_target="tpu_custom_call" | custom-call | tf_op jit(solution)/shard_map/pack_x/pallas_call | solution.py:129
  4.5 2.1 %collective-permute-start = (bf16[128,4352]{1,0:T(8,128)(2,1)S(1)}, bf16[128,4352]{1,0:T(8,128)(2,1)S(1)}, u32[]{:S(2)}, u32[]{:S(2)}) collective-permute-start(bf16[128,4352]{1,0:T(8,128)(2,1)S(1)} %get-tuple-element.36), channel_id=1, source_target_pairs={{0,16},{16,0},{32,48},{48,32},{1,17},{17,1},{33,49},{49,33},{2,18}... | collective-permute-start | bytes 3342344 | tf_op jit(solution)/shard_map/ppermute | solution.py:36
  6.6 1.8 collective-permute-start.1
  8.4 2.0 %pack_y.1 = (bf16[128,3584]{1,0:T(8,128)(2,1)S(1)}, bf16[128,3584]{1,0:T(8,128)(2,1)S(1)}) custom-call(s32[41]{0:T(128)S(1)} %concatenate.30.place, bf16[128,18432]{1,0:T(8,128)(2,1)} %d.5, bf16[128,512]{1,0:T(8,128)(2,1)S(1)} %copy-done), custom_call_target="tpu_custom_call" | custom-call | tf_op jit(solution)/shard_map/pack_y/pallas_call | solution.py:129
  10.4 1.4 collective-permute-start.6
  11.8 1.9 %collective-permute-start.7 = (bf16[128,3584]{1,0:T(8,128)(2,1)S(1)}, bf16[128,3584]{1,0:T(8,128)(2,1)S(1)}, u32[]{:S(2)}, u32[]{:S(2)}) collective-permute-start(bf16[128,3584]{1,0:T(8,128)(2,1)S(1)} %get-tuple-element.40), channel_id=1, source_target_pairs={{0,6},{2,4},{4,2},{6,0},{1,7},{3,5},{5,3},{7,1},{8,14},{10,12},{12... | collective-permute-start | bytes 2752520 | tf_op jit(solution)/shard_map/ppermute | solution.py:36
  13.7 1.7 collective-permute-start.8
  15.5 14.1 %collective-permute-done.near1 = bf16[128,4352]{1,0:T(8,128)(2,1)S(1)} collective-permute-done((bf16[128,4352]{1,0:T(8,128)(2,1)S(1)}, bf16[128,4352]{1,0:T(8,128)(2,1)S(1)}, u32[]{:S(2)}, u32[]{:S(2)}) %collective-permute-start) | collective-permute-done | bytes 1114144 | tf_op jit(solution)/shard_map/ppermute | solution.py:36
  29.6 3.8 %collective-permute-start.2 = (bf16[128,1536]{1,0:T(8,128)(2,1)S(1)}, bf16[128,1536]{1,0:T(8,128)(2,1)S(1)}, u32[]{:S(2)}, u32[]{:S(2)}) collective-permute-start(bf16[128,1536]{1,0:T(8,128)(2,1)S(1)} %slice.40), channel_id=1, source_target_pairs={{0,48},{16,32},{32,16},{48,0},{1,49},{17,33},{33,17},{49,1},{2,50}... | collective-permute-start | bytes 1179656 | tf_op jit(solution)/shard_map/ppermute | solution.py:36
  33.7 2.8 %collective-permute-start.9 = (bf16[128,1280]{1,0:T(8,128)(2,1)S(1)}, bf16[128,1280]{1,0:T(8,128)(2,1)S(1)}, u32[]{:S(2)}, u32[]{:S(2)}) collective-permute-start(bf16[128,1280]{1,0:T(8,128)(2,1)S(1)} %slice.42), channel_id=1, source_target_pairs={{0,6},{2,4},{4,2},{6,0},{1,7},{3,5},{5,3},{7,1},{8,14},{10,12},{12... | collective-permute-start | bytes 983048 | tf_op jit(solution)/shard_map/ppermute | solution.py:36
  36.5 1.9 %pack_own.1.own = bf16[128,4608]{1,0:T(8,128)(2,1)S(1)} custom-call(s32[41]{0:T(128)S(1)} %concatenate.30.place, bf16[128,18432]{1,0:T(8,128)(2,1)} %d.5), custom_call_target="tpu_custom_call" | custom-call | tf_op jit(solution)/shard_map/pack_own/pallas_call | solution.py:129
  38.5 2.6 %collective-permute-done.2.far1 = bf16[128,1536]{1,0:T(8,128)(2,1)S(1)} collective-permute-done((bf16[128,1536]{1,0:T(8,128)(2,1)S(1)}, bf16[128,1536]{1,0:T(8,128)(2,1)S(1)}, u32[]{:S(2)}, u32[]{:S(2)}) %collective-permute-start.2) | collective-permute-done | bytes 393248 | tf_op jit(solution)/shard_map/ppermute | solution.py:36
  41.1 1.2 collective-permute-done.3.far3
  43.2 2.8 %collective-permute-start.4 = (bf16[512,1280]{1,0:T(8,128)(2,1)S(1)}, bf16[512,1280]{1,0:T(8,128)(2,1)S(1)}, u32[]{:S(2)}, u32[]{:S(2)}) collective-permute-start(bf16[512,1280]{1,0:T(8,128)(2,1)S(1)} %partials.5), channel_id=1, source_target_pairs={{0,8},{8,0},{1,9},{9,1},{2,10},{10,2},{3,11},{11,3},{4,12},{12,4},... | collective-permute-start | bytes 3932168 | tf_op jit(solution)/shard_map/ppermute | solution.py:36
  48.2 2.0 %collective-permute-done.11.far = bf16[512,1024]{1,0:T(8,128)(2,1)S(1)} collective-permute-done((bf16[512,1024]{1,0:T(8,128)(2,1)S(1)}, bf16[512,1024]{1,0:T(8,128)(2,1)S(1)}, u32[]{:S(2)}, u32[]{:S(2)}) %collective-permute-start.11) | collective-permute-done | bytes 1048608 | tf_op jit(solution)/shard_map/ppermute | solution.py:36
  54.5 1.9 %collective-permute-start.13 = (bf16[128,1280]{1,0:T(8,128)(2,1)S(1)}, bf16[128,1280]{1,0:T(8,128)(2,1)S(1)}, u32[]{:S(2)}, u32[]{:S(2)}) collective-permute-start(bf16[128,1280]{1,0:T(8,128)(2,1)S(1)} %get-tuple-element.44), channel_id=1, source_target_pairs={{0,6},{2,4},{4,2},{6,0},{1,7},{3,5},{5,3},{7,1},{8,14},{10,12},{12... | collective-permute-start | bytes 983048 | tf_op jit(solution)/shard_map/ppermute | solution.py:36
  57.4 1.3 collective-permute-start.14
  58.8 2.0 %collective-permute-start.16 = (bf16[512,256]{1,0:T(8,128)(2,1)S(1)}, bf16[512,256]{1,0:T(8,128)(2,1)S(1)}, u32[]{:S(2)}, u32[]{:S(2)}) collective-permute-start(bf16[512,256]{1,0:T(8,128)(2,1)S(1)} %get-tuple-element.47), channel_id=1, source_target_pairs={{0,32},{16,48},{32,0},{48,16},{1,33},{17,49},{33,1},{49,17},{2,34}... | collective-permute-start | bytes 786440 | tf_op jit(solution)/shard_map/ppermute | solution.py:36
  60.8 9.9 %collective-permute-done.14.rx3 = bf16[512,256]{1,0:T(8,128)(2,1)S(1)} collective-permute-done((bf16[512,256]{1,0:T(8,128)(2,1)S(1)}, bf16[512,256]{1,0:T(8,128)(2,1)S(1)}, u32[]{:S(2)}, u32[]{:S(2)}) %collective-permute-start.14) | collective-permute-done | bytes 262176 | tf_op jit(solution)/shard_map/ppermute | solution.py:36
  72.5 8.2 %all-to-all-start = ((bf16[8,96,512]{2,1,0:T(8,128)(2,1)}), bf16[8,96,512]{2,1,0:T(8,128)(2,1)S(1)}, u32[]{:S(2)}, u32[]{:S(2)}) async-start(bf16[8,96,512]{2,1,0:T(8,128)(2,1)} %bitcast.7), calls=%async_computation | async-start | bytes 1572864 | tf_op jit(solution)/shard_map/all_to_all | solution.py:496
  80.6 2.2 %collective-permute-start.19 = (bf16[8,64,512]{2,1,0:T(8,128)(2,1)S(1)}, bf16[8,64,512]{2,1,0:T(8,128)(2,1)S(1)}, u32[]{:S(2)}, u32[]{:S(2)}) collective-permute-start(bf16[8,64,512]{2,1,0:T(8,128)(2,1)S(1)} %pad_maximum_fusion.s0), channel_id=1, source_target_pairs={{0,4},{2,6},{4,0},{6,2},{1,5},{3,7},{5,1},{7,3},{8,12},{10,14},{12... | collective-permute-start | bytes 1572872 | tf_op jit(solution)/shard_map/ppermute | solution.py:36
  82.9 1.6 collective-permute-start.20
  84.5 18.2 %all-to-all-done.arrived = bf16[8,96,512]{2,1,0:T(8,128)(2,1)S(1)} async-done(((bf16[8,96,512]{2,1,0:T(8,128)(2,1)}), bf16[8,96,512]{2,1,0:T(8,128)(2,1)S(1)}, u32[]{:S(2)}, u32[]{:S(2)}) %all-to-all-start) | async-done | bytes 786464 | tf_op jit(solution)/shard_map/all_to_all | solution.py:496
  102.9 3.8 %collective-permute-start.25 = (bf16[32,512]{1,0:T(8,128)(2,1)S(1)}, bf16[32,512]{1,0:T(8,128)(2,1)S(1)}, u32[]{:S(2)}, u32[]{:S(2)}) collective-permute-start(bf16[32,512]{1,0:T(8,128)(2,1)S(1)} %slice.46), channel_id=1, source_target_pairs={{0,9},{1,8},{8,1},{9,0},{2,11},{3,10},{10,3},{11,2},{4,13},{5,12},... | collective-permute-start | bytes 98312 | tf_op jit(solution)/shard_map/ppermute | solution.py:503
  106.7 3.2 %collective-permute-start.24 = (bf16[32,512]{1,0:T(8,128)(2,1)S(1)}, bf16[32,512]{1,0:T(8,128)(2,1)S(1)}, u32[]{:S(2)}, u32[]{:S(2)}) collective-permute-start(bf16[32,512]{1,0:T(8,128)(2,1)S(1)} %slice.46), channel_id=1, source_target_pairs={{0,8},{8,0},{1,9},{9,1},{2,10},{10,2},{3,11},{11,3},{4,12},{12,4},... | collective-permute-start | bytes 98312 | tf_op jit(solution)/shard_map/ppermute | solution.py:36
  110.8 1.5 collective-permute-start.26
  113.5 1.5 collective-permute-start.28
  115.0 2.8 %collective-permute-start.22 = (bf16[128,512]{1,0:T(8,128)(2,1)S(1)}, bf16[128,512]{1,0:T(8,128)(2,1)S(1)}, u32[]{:S(2)}, u32[]{:S(2)}) collective-permute-start(bf16[128,512]{1,0:T(8,128)(2,1)S(1)} %pad_maximum_fusion.3.r0), channel_id=1, source_target_pairs={{0,4},{2,6},{4,0},{6,2},{1,5},{3,7},{5,1},{7,3},{8,12},{10,14},{12... | collective-permute-start | bytes 393224 | tf_op jit(solution)/shard_map/ppermute | solution.py:36
  119.5 2.7 %collective-permute-done.28.q3 = bf16[128,512]{1,0:T(8,128)(2,1)S(1)} collective-permute-done((bf16[128,512]{1,0:T(8,128)(2,1)S(1)}, bf16[128,512]{1,0:T(8,128)(2,1)S(1)}, u32[]{:S(2)}, u32[]{:S(2)}) %collective-permute-start.28) | collective-permute-done | bytes 131104 | tf_op jit(solution)/shard_map/ppermute | solution.py:36
  122.9 3.2 %collective-permute-start.30 = (bf16[128,512]{1,0:T(8,128)(2,1)S(1)}, bf16[128,512]{1,0:T(8,128)(2,1)S(1)}, u32[]{:S(2)}, u32[]{:S(2)}) collective-permute-start(bf16[128,512]{1,0:T(8,128)(2,1)S(1)} %choose.1.r0), channel_id=1, source_target_pairs={{0,4},{2,6},{4,0},{6,2},{1,5},{3,7},{5,1},{7,3},{8,12},{10,14},{12... | collective-permute-start | bytes 393224 | tf_op jit(solution)/shard_map/ppermute | solution.py:36
  127.5 3.9 %roots.2 = (bf16[64,512]{1,0:T(8,128)(2,1)S(1)}, f32[64,512]{1,0:T(8,128)S(1)}, f32[64,512]{1,0:T(8,128)S(1)}) custom-call(s32[41]{0:T(128)S(1)} %concatenate.30.place, bf16[128,512]{1,0:T(8,128)(2,1)S(1)} %pad_maximum_fusion.3.r0, bf16[128,512]{1,0:T(8,128)(2,1)S(1)} %collective-permute-done.21.r1, bf16[128,512]{1,0:T(8,128)(2,1)S(1)} %collective-permute-done.22.r2, ...), custom_call_target="tpu_custom_call" | custom-call | tf_op jit(solution)/shard_map/roots/pallas_call | solution.py:402
  131.8 2.5 %collective-permute-done.31.r3 = bf16[128,512]{1,0:T(8,128)(2,1)S(1)} collective-permute-done((bf16[128,512]{1,0:T(8,128)(2,1)S(1)}, bf16[128,512]{1,0:T(8,128)(2,1)S(1)}, u32[]{:S(2)}, u32[]{:S(2)}) %collective-permute-start.31) | collective-permute-done | bytes 131104 | tf_op jit(solution)/shard_map/ppermute | solution.py:36
  134.3 1.8 collective-permute-start.33
  136.1 3.9 %collective-permute-start.32 = (bf16[64,512]{1,0:T(8,128)(2,1)S(1)}, bf16[64,512]{1,0:T(8,128)(2,1)S(1)}, u32[]{:S(2)}, u32[]{:S(2)}) collective-permute-start(bf16[64,512]{1,0:T(8,128)(2,1)S(1)} %get-tuple-element.58), channel_id=1, source_target_pairs={{0,64},{64,0},{128,192},{192,128},{1,65},{65,1},{129,193},{193,129... | collective-permute-start | bytes 196616 | tf_op jit(solution)/shard_map/ppermute | solution.py:36
  140.0 4.5 %roots.3 = (bf16[64,512]{1,0:T(8,128)(2,1)S(1)}, f32[2,64,512]{2,1,0:T(8,128)}, f32[2,64,512]{2,1,0:T(8,128)}) custom-call(s32[41]{0:T(128)S(1)} %concatenate.30.place, bf16[128,512]{1,0:T(8,128)(2,1)S(1)} %choose.1.r0, bf16[128,512]{1,0:T(8,128)(2,1)S(1)} %collective-permute-done.29.r1, bf16[128,512]{1,0:T(8,128)(2,1)S(1)} %collective-permute-done.30.r2, ...), custom_call_target="tpu_custom_call" | custom-call | tf_op jit(solution)/shard_map/roots/pallas_call | solution.py:402
  144.5 1.8 %collective-permute-done.32 = bf16[64,512]{1,0:T(8,128)(2,1)S(1)} collective-permute-done((bf16[64,512]{1,0:T(8,128)(2,1)S(1)}, bf16[64,512]{1,0:T(8,128)(2,1)S(1)}, u32[]{:S(2)}, u32[]{:S(2)}) %collective-permute-start.32) | collective-permute-done | bytes 65568 | tf_op jit(solution)/shard_map/ppermute | solution.py:36
  146.4 1.5 collective-permute-start.36
  149.0 4.6 %collective-permute-start.39 = (bf16[64,512]{1,0:T(8,128)(2,1)S(1)}, bf16[64,512]{1,0:T(8,128)(2,1)S(1)}, u32[]{:S(2)}, u32[]{:S(2)}) collective-permute-start(bf16[64,512]{1,0:T(8,128)(2,1)S(1)} %get-tuple-element.66), channel_id=1, source_target_pairs={{0,192},{64,128},{128,64},{192,0},{1,193},{65,129},{129,65},{193,1... | collective-permute-start | bytes 196616 | tf_op jit(solution)/shard_map/ppermute | solution.py:36
  153.8 1.3 collective-permute-done.36
  155.7 2.2 %collective-permute-done.39 = bf16[64,512]{1,0:T(8,128)(2,1)S(1)} collective-permute-done((bf16[64,512]{1,0:T(8,128)(2,1)S(1)}, bf16[64,512]{1,0:T(8,128)(2,1)S(1)}, u32[]{:S(2)}, u32[]{:S(2)}) %collective-permute-start.39) | collective-permute-done | bytes 65568 | tf_op jit(solution)/shard_map/ppermute | solution.py:36
  158.0 1.7 collective-permute-start.43
  160.5 1.2 collective-permute-start.41
  161.8 1.4 collective-permute-start.42
  163.2 7.3 %collective-permute-done.40.refs_1_ = bf16[384,512]{1,0:T(8,128)(2,1)S(1)} collective-permute-done((bf16[384,512]{1,0:T(8,128)(2,1)S(1)}, bf16[384,512]{1,0:T(8,128)(2,1)S(1)}, u32[]{:S(2)}, u32[]{:S(2)}) %collective-permute-start.40) | collective-permute-done | bytes 393248 | tf_op jit(solution)/shard_map/ppermute | solution.py:36
  170.5 1.2 collective-permute-start.44
  171.7 6.2 %collective-permute-done.41.refs_2_ = bf16[384,512]{1,0:T(8,128)(2,1)S(1)} collective-permute-done((bf16[384,512]{1,0:T(8,128)(2,1)S(1)}, bf16[384,512]{1,0:T(8,128)(2,1)S(1)}, u32[]{:S(2)}, u32[]{:S(2)}) %collective-permute-start.41) | collective-permute-done | bytes 393248 | tf_op jit(solution)/shard_map/ppermute | solution.py:36
  179.0 1.7 collective-permute-done.46.refs_7_
  180.7 2.0 %put_blocks.1 = bf16[64,18432]{1,0:T(8,128)(2,1)} custom-call(s32[41]{0:T(128)S(1)} %concatenate.30.place, bf16[1024,512]{1,0:T(8,128)(2,1)S(1)} %get-tuple-element.70.refs_0_, bf16[384,512]{1,0:T(8,128)(2,1)S(1)} %collective-permute-done.40.refs_1_, bf16[384,512]{1,0:T(8,128)(2,1)S(1)} %collective-permute-done.41.refs_2_, ...), custom_call_target="tpu_custom_call" | custom-call | tf_op jit(solution)/shard_map/put_blocks/pallas_call | solution.py:453
  (97 shorter events, 22.4 us)
Async XLA Ops:
  4.5 25.1 %collective-permute-start = (bf16[128,4352]{1,0:T(8,128)(2,1)S(1)}, bf16[128,4352]{1,0:T(8,128)(2,1)S(1)}, u32[]{:S(2)}, u32[]{:S(2)}) collective-permute-start(bf16[128,4352]{1,0:T(8,128)(2,1)S(1)} %get-tuple-element.36), channel_id=1, source_target_pairs={{0,16},{16,0},{32,48},{48,32},{1,17},{17,1},{33,49},{49,33},{2,18}... | collective-permute-start | bytes 3342344 | tf_op jit(solution)/shard_map/ppermute | solution.py:36
  6.6 26.8 %collective-permute-start.1 = (bf16[128,4352]{1,0:T(8,128)(2,1)S(1)}, bf16[128,4352]{1,0:T(8,128)(2,1)S(1)}, u32[]{:S(2)}, u32[]{:S(2)}) collective-permute-start(bf16[128,4352]{1,0:T(8,128)(2,1)S(1)} %get-tuple-element.37), channel_id=1, source_target_pairs={{0,48},{16,32},{32,16},{48,0},{1,49},{17,33},{33,17},{49,1},{2,50}... | collective-permute-start | bytes 3342344 | tf_op jit(solution)/shard_map/ppermute | solution.py:36
  10.4 23.2 %collective-permute-start.6 = (bf16[128,3584]{1,0:T(8,128)(2,1)S(1)}, bf16[128,3584]{1,0:T(8,128)(2,1)S(1)}, u32[]{:S(2)}, u32[]{:S(2)}) collective-permute-start(bf16[128,3584]{1,0:T(8,128)(2,1)S(1)} %get-tuple-element.39), channel_id=1, source_target_pairs={{0,2},{2,0},{4,6},{6,4},{1,3},{3,1},{5,7},{7,5},{8,10},{10,8},{12,... | collective-permute-start | bytes 2752520 | tf_op jit(solution)/shard_map/ppermute | solution.py:36
  11.8 21.9 %collective-permute-start.7 = (bf16[128,3584]{1,0:T(8,128)(2,1)S(1)}, bf16[128,3584]{1,0:T(8,128)(2,1)S(1)}, u32[]{:S(2)}, u32[]{:S(2)}) collective-permute-start(bf16[128,3584]{1,0:T(8,128)(2,1)S(1)} %get-tuple-element.40), channel_id=1, source_target_pairs={{0,6},{2,4},{4,2},{6,0},{1,7},{3,5},{5,3},{7,1},{8,14},{10,12},{12... | collective-permute-start | bytes 2752520 | tf_op jit(solution)/shard_map/ppermute | solution.py:36
  13.7 19.8 %collective-permute-start.8 = (bf16[4,64,512]{2,1,0:T(8,128)(2,1)S(1)}, bf16[4,64,512]{2,1,0:T(8,128)(2,1)S(1)}, u32[]{:S(2)}, u32[]{:S(2)}) collective-permute-start(bf16[4,64,512]{2,1,0:T(8,128)(2,1)S(1)} %cast_rows.1), channel_id=1, source_target_pairs={{0,1},{1,0},{2,3},{3,2},{4,5},{5,4},{6,7},{7,6},{8,9},{9,8},{10,11... | collective-permute-start | bytes 786440 | tf_op jit(solution)/shard_map/ppermute | solution.py:36
  29.6 11.5 %collective-permute-start.2 = (bf16[128,1536]{1,0:T(8,128)(2,1)S(1)}, bf16[128,1536]{1,0:T(8,128)(2,1)S(1)}, u32[]{:S(2)}, u32[]{:S(2)}) collective-permute-start(bf16[128,1536]{1,0:T(8,128)(2,1)S(1)} %slice.40), channel_id=1, source_target_pairs={{0,48},{16,32},{32,16},{48,0},{1,49},{17,33},{33,17},{49,1},{2,50}... | collective-permute-start | bytes 1179656 | tf_op jit(solution)/shard_map/ppermute | solution.py:36
  33.5 8.9 %collective-permute-start.3 = (bf16[128,1536]{1,0:T(8,128)(2,1)S(1)}, bf16[128,1536]{1,0:T(8,128)(2,1)S(1)}, u32[]{:S(2)}, u32[]{:S(2)}) collective-permute-start(bf16[128,1536]{1,0:T(8,128)(2,1)S(1)} %slice.41), channel_id=1, source_target_pairs={{0,16},{16,0},{32,48},{48,32},{1,17},{17,1},{33,49},{49,33},{2,18}... | collective-permute-start | bytes 1179656 | tf_op jit(solution)/shard_map/ppermute | solution.py:36
  33.7 12.4 %collective-permute-start.9 = (bf16[128,1280]{1,0:T(8,128)(2,1)S(1)}, bf16[128,1280]{1,0:T(8,128)(2,1)S(1)}, u32[]{:S(2)}, u32[]{:S(2)}) collective-permute-start(bf16[128,1280]{1,0:T(8,128)(2,1)S(1)} %slice.42), channel_id=1, source_target_pairs={{0,6},{2,4},{4,2},{6,0},{1,7},{3,5},{5,3},{7,1},{8,14},{10,12},{12... | collective-permute-start | bytes 983048 | tf_op jit(solution)/shard_map/ppermute | solution.py:36
  36.5 9.6 %collective-permute-start.10 = (bf16[128,1280]{1,0:T(8,128)(2,1)S(1)}, bf16[128,1280]{1,0:T(8,128)(2,1)S(1)}, u32[]{:S(2)}, u32[]{:S(2)}) collective-permute-start(bf16[128,1280]{1,0:T(8,128)(2,1)S(1)} %slice.43), channel_id=1, source_target_pairs={{0,2},{2,0},{4,6},{6,4},{1,3},{3,1},{5,7},{7,5},{8,10},{10,8},{12,... | collective-permute-start | bytes 983048 | tf_op jit(solution)/shard_map/ppermute | solution.py:36
  43.2 9.9 %collective-permute-start.4 = (bf16[512,1280]{1,0:T(8,128)(2,1)S(1)}, bf16[512,1280]{1,0:T(8,128)(2,1)S(1)}, u32[]{:S(2)}, u32[]{:S(2)}) collective-permute-start(bf16[512,1280]{1,0:T(8,128)(2,1)S(1)} %partials.5), channel_id=1, source_target_pairs={{0,8},{8,0},{1,9},{9,1},{2,10},{10,2},{3,11},{11,3},{4,12},{12,4},... | collective-permute-start | bytes 3932168 | tf_op jit(solution)/shard_map/ppermute | solution.py:36
  46.8 3.4 %collective-permute-start.11 = (bf16[512,1024]{1,0:T(8,128)(2,1)S(1)}, bf16[512,1024]{1,0:T(8,128)(2,1)S(1)}, u32[]{:S(2)}, u32[]{:S(2)}) collective-permute-start(bf16[512,1024]{1,0:T(8,128)(2,1)S(1)} %partials.7), channel_id=1, source_target_pairs={{0,8},{8,0},{1,9},{9,1},{2,10},{10,2},{3,11},{11,3},{4,12},{12,4},... | collective-permute-start | bytes 3145736 | tf_op jit(solution)/shard_map/ppermute | solution.py:36
  51.2 7.6 %collective-permute-start.12 = (bf16[512,256]{1,0:T(8,128)(2,1)S(1)}, bf16[512,256]{1,0:T(8,128)(2,1)S(1)}, u32[]{:S(2)}, u32[]{:S(2)}) collective-permute-start(bf16[512,256]{1,0:T(8,128)(2,1)S(1)} %get-tuple-element.43), channel_id=1, source_target_pairs={{0,16},{16,0},{32,48},{48,32},{1,17},{17,1},{33,49},{49,33},{2,18}... | collective-permute-start | bytes 786440 | tf_op jit(solution)/shard_map/ppermute | solution.py:36
  54.0 16.7 %collective-permute-start.5 = (bf16[128,1280]{1,0:T(8,128)(2,1)S(1)}, bf16[128,1280]{1,0:T(8,128)(2,1)S(1)}, u32[]{:S(2)}, u32[]{:S(2)}) collective-permute-start(bf16[128,1280]{1,0:T(8,128)(2,1)S(1)} %get-tuple-element.38), channel_id=1, source_target_pairs={{0,2},{2,0},{4,6},{6,4},{1,3},{3,1},{5,7},{7,5},{8,10},{10,8},{12,... | collective-permute-start | bytes 983048 | tf_op jit(solution)/shard_map/ppermute | solution.py:36
  54.5 16.2 %collective-permute-start.13 = (bf16[128,1280]{1,0:T(8,128)(2,1)S(1)}, bf16[128,1280]{1,0:T(8,128)(2,1)S(1)}, u32[]{:S(2)}, u32[]{:S(2)}) collective-permute-start(bf16[128,1280]{1,0:T(8,128)(2,1)S(1)} %get-tuple-element.44), channel_id=1, source_target_pairs={{0,6},{2,4},{4,2},{6,0},{1,7},{3,5},{5,3},{7,1},{8,14},{10,12},{12... | collective-permute-start | bytes 983048 | tf_op jit(solution)/shard_map/ppermute | solution.py:36
  56.4 14.9 %collective-permute-start.15 = (bf16[128,1280]{1,0:T(8,128)(2,1)S(1)}, bf16[128,1280]{1,0:T(8,128)(2,1)S(1)}, u32[]{:S(2)}, u32[]{:S(2)}) collective-permute-start(bf16[128,1280]{1,0:T(8,128)(2,1)S(1)} %get-tuple-element.46), channel_id=1, source_target_pairs={{0,4},{2,6},{4,0},{6,2},{1,5},{3,7},{5,1},{7,3},{8,12},{10,14},{12... | collective-permute-start | bytes 983048 | tf_op jit(solution)/shard_map/ppermute | solution.py:36
  57.4 13.3 %collective-permute-start.14 = (bf16[512,256]{1,0:T(8,128)(2,1)S(1)}, bf16[512,256]{1,0:T(8,128)(2,1)S(1)}, u32[]{:S(2)}, u32[]{:S(2)}) collective-permute-start(bf16[512,256]{1,0:T(8,128)(2,1)S(1)} %get-tuple-element.45), channel_id=1, source_target_pairs={{0,48},{16,32},{32,16},{48,0},{1,49},{17,33},{33,17},{49,1},{2,50}... | collective-permute-start | bytes 786440 | tf_op jit(solution)/shard_map/ppermute | solution.py:36
  58.8 11.9 %collective-permute-start.16 = (bf16[512,256]{1,0:T(8,128)(2,1)S(1)}, bf16[512,256]{1,0:T(8,128)(2,1)S(1)}, u32[]{:S(2)}, u32[]{:S(2)}) collective-permute-start(bf16[512,256]{1,0:T(8,128)(2,1)S(1)} %get-tuple-element.47), channel_id=1, source_target_pairs={{0,32},{16,48},{32,0},{48,16},{1,33},{17,49},{33,1},{49,17},{2,34}... | collective-permute-start | bytes 786440 | tf_op jit(solution)/shard_map/ppermute | solution.py:36
  72.5 30.2 %all-to-all-start = ((bf16[8,96,512]{2,1,0:T(8,128)(2,1)}), bf16[8,96,512]{2,1,0:T(8,128)(2,1)S(1)}, u32[]{:S(2)}, u32[]{:S(2)}) async-start(bf16[8,96,512]{2,1,0:T(8,128)(2,1)} %bitcast.7), calls=%async_computation | async-start | bytes 1572864 | tf_op jit(solution)/shard_map/all_to_all | solution.py:496
  80.6 32.9 %collective-permute-start.18 = (bf16[8,64,512]{2,1,0:T(8,128)(2,1)S(1)}, bf16[8,64,512]{2,1,0:T(8,128)(2,1)S(1)}, u32[]{:S(2)}, u32[]{:S(2)}) collective-permute-start(bf16[8,64,512]{2,1,0:T(8,128)(2,1)S(1)} %pad_maximum_fusion.s0), channel_id=1, source_target_pairs={{0,2},{2,0},{4,6},{6,4},{1,3},{3,1},{5,7},{7,5},{8,10},{10,8},{12,... | collective-permute-start | bytes 1572872 | tf_op jit(solution)/shard_map/ppermute | solution.py:36
  80.6 34.3 %collective-permute-start.19 = (bf16[8,64,512]{2,1,0:T(8,128)(2,1)S(1)}, bf16[8,64,512]{2,1,0:T(8,128)(2,1)S(1)}, u32[]{:S(2)}, u32[]{:S(2)}) collective-permute-start(bf16[8,64,512]{2,1,0:T(8,128)(2,1)S(1)} %pad_maximum_fusion.s0), channel_id=1, source_target_pairs={{0,4},{2,6},{4,0},{6,2},{1,5},{3,7},{5,1},{7,3},{8,12},{10,14},{12... | collective-permute-start | bytes 1572872 | tf_op jit(solution)/shard_map/ppermute | solution.py:36
  82.9 32.1 %collective-permute-start.20 = (bf16[8,64,512]{2,1,0:T(8,128)(2,1)S(1)}, bf16[8,64,512]{2,1,0:T(8,128)(2,1)S(1)}, u32[]{:S(2)}, u32[]{:S(2)}) collective-permute-start(bf16[8,64,512]{2,1,0:T(8,128)(2,1)S(1)} %pad_maximum_fusion.s0), channel_id=1, source_target_pairs={{0,6},{2,4},{4,2},{6,0},{1,7},{3,5},{5,3},{7,1},{8,14},{10,12},{12... | collective-permute-start | bytes 1572872 | tf_op jit(solution)/shard_map/ppermute | solution.py:36
  102.8 3.9 %collective-permute-start.17 = (bf16[96,512]{1,0:T(8,128)(2,1)S(1)}, bf16[96,512]{1,0:T(8,128)(2,1)S(1)}, u32[]{:S(2)}, u32[]{:S(2)}) collective-permute-start(bf16[96,512]{1,0:T(8,128)(2,1)S(1)} %line_sum.1), channel_id=1, source_target_pairs={{0,1},{1,0},{2,3},{3,2},{4,5},{5,4},{6,7},{7,6},{8,9},{9,8},{10,11... | collective-permute-start | bytes 294920 | tf_op jit(solution)/shard_map/ppermute | solution.py:36
  102.9 7.1 %collective-permute-start.25 = (bf16[32,512]{1,0:T(8,128)(2,1)S(1)}, bf16[32,512]{1,0:T(8,128)(2,1)S(1)}, u32[]{:S(2)}, u32[]{:S(2)}) collective-permute-start(bf16[32,512]{1,0:T(8,128)(2,1)S(1)} %slice.46), channel_id=1, source_target_pairs={{0,9},{1,8},{8,1},{9,0},{2,11},{3,10},{10,3},{11,2},{4,13},{5,12},... | collective-permute-start | bytes 98312 | tf_op jit(solution)/shard_map/ppermute | solution.py:503
  106.7 4.1 %collective-permute-start.24 = (bf16[32,512]{1,0:T(8,128)(2,1)S(1)}, bf16[32,512]{1,0:T(8,128)(2,1)S(1)}, u32[]{:S(2)}, u32[]{:S(2)}) collective-permute-start(bf16[32,512]{1,0:T(8,128)(2,1)S(1)} %slice.46), channel_id=1, source_target_pairs={{0,8},{8,0},{1,9},{9,1},{2,10},{10,2},{3,11},{11,3},{4,12},{12,4},... | collective-permute-start | bytes 98312 | tf_op jit(solution)/shard_map/ppermute | solution.py:36
  110.8 7.0 %collective-permute-start.26 = (bf16[128,512]{1,0:T(8,128)(2,1)S(1)}, bf16[128,512]{1,0:T(8,128)(2,1)S(1)}, u32[]{:S(2)}, u32[]{:S(2)}) collective-permute-start(bf16[128,512]{1,0:T(8,128)(2,1)S(1)} %pad_maximum_fusion.4.q0), channel_id=1, source_target_pairs={{0,16},{16,0},{32,48},{48,32},{1,17},{17,1},{33,49},{49,33},{2,18}... | collective-permute-start | bytes 393224 | tf_op jit(solution)/shard_map/ppermute | solution.py:36
  112.3 7.2 %collective-permute-start.27 = (bf16[128,512]{1,0:T(8,128)(2,1)S(1)}, bf16[128,512]{1,0:T(8,128)(2,1)S(1)}, u32[]{:S(2)}, u32[]{:S(2)}) collective-permute-start(bf16[128,512]{1,0:T(8,128)(2,1)S(1)} %pad_maximum_fusion.4.q0), channel_id=1, source_target_pairs={{0,32},{16,48},{32,0},{48,16},{1,33},{17,49},{33,1},{49,17},{2,34}... | collective-permute-start | bytes 393224 | tf_op jit(solution)/shard_map/ppermute | solution.py:36
  113.5 8.7 %collective-permute-start.28 = (bf16[128,512]{1,0:T(8,128)(2,1)S(1)}, bf16[128,512]{1,0:T(8,128)(2,1)S(1)}, u32[]{:S(2)}, u32[]{:S(2)}) collective-permute-start(bf16[128,512]{1,0:T(8,128)(2,1)S(1)} %pad_maximum_fusion.4.q0), channel_id=1, source_target_pairs={{0,48},{16,32},{32,16},{48,0},{1,49},{17,33},{33,17},{49,1},{2,50}... | collective-permute-start | bytes 393224 | tf_op jit(solution)/shard_map/ppermute | solution.py:36
  115.0 11.1 %collective-permute-start.21 = (bf16[128,512]{1,0:T(8,128)(2,1)S(1)}, bf16[128,512]{1,0:T(8,128)(2,1)S(1)}, u32[]{:S(2)}, u32[]{:S(2)}) collective-permute-start(bf16[128,512]{1,0:T(8,128)(2,1)S(1)} %pad_maximum_fusion.3.r0), channel_id=1, source_target_pairs={{0,2},{2,0},{4,6},{6,4},{1,3},{3,1},{5,7},{7,5},{8,10},{10,8},{12,... | collective-permute-start | bytes 393224 | tf_op jit(solution)/shard_map/ppermute | solution.py:36
  115.0 12.5 %collective-permute-start.22 = (bf16[128,512]{1,0:T(8,128)(2,1)S(1)}, bf16[128,512]{1,0:T(8,128)(2,1)S(1)}, u32[]{:S(2)}, u32[]{:S(2)}) collective-permute-start(bf16[128,512]{1,0:T(8,128)(2,1)S(1)} %pad_maximum_fusion.3.r0), channel_id=1, source_target_pairs={{0,4},{2,6},{4,0},{6,2},{1,5},{3,7},{5,1},{7,3},{8,12},{10,14},{12... | collective-permute-start | bytes 393224 | tf_op jit(solution)/shard_map/ppermute | solution.py:36
  117.8 9.7 %collective-permute-start.23 = (bf16[128,512]{1,0:T(8,128)(2,1)S(1)}, bf16[128,512]{1,0:T(8,128)(2,1)S(1)}, u32[]{:S(2)}, u32[]{:S(2)}) collective-permute-start(bf16[128,512]{1,0:T(8,128)(2,1)S(1)} %pad_maximum_fusion.3.r0), channel_id=1, source_target_pairs={{0,6},{2,4},{4,2},{6,0},{1,7},{3,5},{5,3},{7,1},{8,14},{10,12},{12... | collective-permute-start | bytes 393224 | tf_op jit(solution)/shard_map/ppermute | solution.py:36
  122.8 8.6 %collective-permute-start.29 = (bf16[128,512]{1,0:T(8,128)(2,1)S(1)}, bf16[128,512]{1,0:T(8,128)(2,1)S(1)}, u32[]{:S(2)}, u32[]{:S(2)}) collective-permute-start(bf16[128,512]{1,0:T(8,128)(2,1)S(1)} %choose.1.r0), channel_id=1, source_target_pairs={{0,2},{2,0},{4,6},{6,4},{1,3},{3,1},{5,7},{7,5},{8,10},{10,8},{12,... | collective-permute-start | bytes 393224 | tf_op jit(solution)/shard_map/ppermute | solution.py:36
  122.9 8.9 %collective-permute-start.30 = (bf16[128,512]{1,0:T(8,128)(2,1)S(1)}, bf16[128,512]{1,0:T(8,128)(2,1)S(1)}, u32[]{:S(2)}, u32[]{:S(2)}) collective-permute-start(bf16[128,512]{1,0:T(8,128)(2,1)S(1)} %choose.1.r0), channel_id=1, source_target_pairs={{0,4},{2,6},{4,0},{6,2},{1,5},{3,7},{5,1},{7,3},{8,12},{10,14},{12... | collective-permute-start | bytes 393224 | tf_op jit(solution)/shard_map/ppermute | solution.py:36
  126.1 8.2 %collective-permute-start.31 = (bf16[128,512]{1,0:T(8,128)(2,1)S(1)}, bf16[128,512]{1,0:T(8,128)(2,1)S(1)}, u32[]{:S(2)}, u32[]{:S(2)}) collective-permute-start(bf16[128,512]{1,0:T(8,128)(2,1)S(1)} %choose.1.r0), channel_id=1, source_target_pairs={{0,6},{2,4},{4,2},{6,0},{1,7},{3,5},{5,3},{7,1},{8,14},{10,12},{12... | collective-permute-start | bytes 393224 | tf_op jit(solution)/shard_map/ppermute | solution.py:36
  134.3 10.2 %collective-permute-start.34 = (bf16[64,512]{1,0:T(8,128)(2,1)S(1)}, bf16[64,512]{1,0:T(8,128)(2,1)S(1)}, u32[]{:S(2)}, u32[]{:S(2)}) collective-permute-start(bf16[64,512]{1,0:T(8,128)(2,1)S(1)} %get-tuple-element.58), channel_id=1, source_target_pairs={{0,192},{64,128},{128,64},{192,0},{1,193},{65,129},{129,65},{193,1... | collective-permute-start | bytes 196616 | tf_op jit(solution)/shard_map/ppermute | solution.py:36
  134.3 10.2 %collective-permute-start.33 = (bf16[64,512]{1,0:T(8,128)(2,1)S(1)}, bf16[64,512]{1,0:T(8,128)(2,1)S(1)}, u32[]{:S(2)}, u32[]{:S(2)}) collective-permute-start(bf16[64,512]{1,0:T(8,128)(2,1)S(1)} %get-tuple-element.58), channel_id=1, source_target_pairs={{0,128},{64,192},{128,0},{192,64},{1,129},{65,193},{129,1},{193,65... | collective-permute-start | bytes 196616 | tf_op jit(solution)/shard_map/ppermute | solution.py:36
  136.1 10.2 %collective-permute-start.32 = (bf16[64,512]{1,0:T(8,128)(2,1)S(1)}, bf16[64,512]{1,0:T(8,128)(2,1)S(1)}, u32[]{:S(2)}, u32[]{:S(2)}) collective-permute-start(bf16[64,512]{1,0:T(8,128)(2,1)S(1)} %get-tuple-element.58), channel_id=1, source_target_pairs={{0,64},{64,0},{128,192},{192,128},{1,65},{65,1},{129,193},{193,129... | collective-permute-start | bytes 196616 | tf_op jit(solution)/shard_map/ppermute | solution.py:36
  146.3 7.5 %collective-permute-start.35 = (bf16[256,512]{1,0:T(8,128)(2,1)S(1)}, bf16[256,512]{1,0:T(8,128)(2,1)S(1)}, u32[]{:S(2)}, u32[]{:S(2)}) collective-permute-start(bf16[256,512]{1,0:T(8,128)(2,1)S(1)} %pad_maximum_fusion.1), channel_id=1, source_target_pairs={{0,16},{16,0},{32,48},{48,32},{1,17},{17,1},{33,49},{49,33},{2,18}... | collective-permute-start | bytes 786440 | tf_op jit(solution)/shard_map/ppermute | solution.py:36
  146.4 8.7 %collective-permute-start.36 = (bf16[256,512]{1,0:T(8,128)(2,1)S(1)}, bf16[256,512]{1,0:T(8,128)(2,1)S(1)}, u32[]{:S(2)}, u32[]{:S(2)}) collective-permute-start(bf16[256,512]{1,0:T(8,128)(2,1)S(1)} %pad_maximum_fusion.1), channel_id=1, source_target_pairs={{0,48},{16,32},{32,16},{48,0},{1,49},{17,33},{33,17},{49,1},{2,50}... | collective-permute-start | bytes 786440 | tf_op jit(solution)/shard_map/ppermute | solution.py:36
  147.9 7.7 %collective-permute-start.37 = (bf16[64,512]{1,0:T(8,128)(2,1)S(1)}, bf16[64,512]{1,0:T(8,128)(2,1)S(1)}, u32[]{:S(2)}, u32[]{:S(2)}) collective-permute-start(bf16[64,512]{1,0:T(8,128)(2,1)S(1)} %get-tuple-element.66), channel_id=1, source_target_pairs={{0,64},{64,0},{128,192},{192,128},{1,65},{65,1},{129,193},{193,129... | collective-permute-start | bytes 196616 | tf_op jit(solution)/shard_map/ppermute | solution.py:36
  147.9 7.7 %collective-permute-start.38 = (bf16[64,512]{1,0:T(8,128)(2,1)S(1)}, bf16[64,512]{1,0:T(8,128)(2,1)S(1)}, u32[]{:S(2)}, u32[]{:S(2)}) collective-permute-start(bf16[64,512]{1,0:T(8,128)(2,1)S(1)} %get-tuple-element.66), channel_id=1, source_target_pairs={{0,128},{64,192},{128,0},{192,64},{1,129},{65,193},{129,1},{193,65... | collective-permute-start | bytes 196616 | tf_op jit(solution)/shard_map/ppermute | solution.py:36
  149.0 8.9 %collective-permute-start.39 = (bf16[64,512]{1,0:T(8,128)(2,1)S(1)}, bf16[64,512]{1,0:T(8,128)(2,1)S(1)}, u32[]{:S(2)}, u32[]{:S(2)}) collective-permute-start(bf16[64,512]{1,0:T(8,128)(2,1)S(1)} %get-tuple-element.66), channel_id=1, source_target_pairs={{0,192},{64,128},{128,64},{192,0},{1,193},{65,129},{129,65},{193,1... | collective-permute-start | bytes 196616 | tf_op jit(solution)/shard_map/ppermute | solution.py:36
  158.0 22.7 %collective-permute-start.43 = (bf16[1024,512]{1,0:T(8,128)(2,1)S(1)}, bf16[1024,512]{1,0:T(8,128)(2,1)S(1)}, u32[]{:S(2)}, u32[]{:S(2)}) collective-permute-start(bf16[1024,512]{1,0:T(8,128)(2,1)S(1)} %get-tuple-element.70.refs_0_), channel_id=1, source_target_pairs={{0,8},{8,0},{1,9},{9,1},{2,10},{10,2},{3,11},{11,3},{4,12},{12,4},... | collective-permute-start | bytes 3145736 | tf_op jit(solution)/shard_map/ppermute | solution.py:36
  159.7 10.8 %collective-permute-start.40 = (bf16[384,512]{1,0:T(8,128)(2,1)S(1)}, bf16[384,512]{1,0:T(8,128)(2,1)S(1)}, u32[]{:S(2)}, u32[]{:S(2)}) collective-permute-start(bf16[384,512]{1,0:T(8,128)(2,1)S(1)} %slice_dynamic-update-slice_fusion.1), channel_id=1, source_target_pairs={{0,16},{16,0},{32,48},{48,32},{1,17},{17,1},{33,49},{49,33},{2,18}... | collective-permute-start | bytes 1179656 | tf_op jit(solution)/shard_map/ppermute | solution.py:36
  160.5 17.3 %collective-permute-start.41 = (bf16[384,512]{1,0:T(8,128)(2,1)S(1)}, bf16[384,512]{1,0:T(8,128)(2,1)S(1)}, u32[]{:S(2)}, u32[]{:S(2)}) collective-permute-start(bf16[384,512]{1,0:T(8,128)(2,1)S(1)} %slice_dynamic-update-slice_fusion), channel_id=1, source_target_pairs={{0,48},{16,32},{32,16},{48,0},{1,49},{17,33},{33,17},{49,1},{2,50}... | collective-permute-start | bytes 1179656 | tf_op jit(solution)/shard_map/ppermute | solution.py:36
  161.8 17.2 %collective-permute-start.42 = (bf16[256,512]{1,0:T(8,128)(2,1)S(1)}, bf16[256,512]{1,0:T(8,128)(2,1)S(1)}, u32[]{:S(2)}, u32[]{:S(2)}) collective-permute-start(bf16[256,512]{1,0:T(8,128)(2,1)S(1)} %pad_maximum_fusion.2), channel_id=1, source_target_pairs={{0,32},{16,48},{32,0},{48,16},{1,33},{17,49},{33,1},{49,17},{2,34}... | collective-permute-start | bytes 786440 | tf_op jit(solution)/shard_map/ppermute | solution.py:36
  170.5 10.2 %collective-permute-start.44 = (bf16[384,512]{1,0:T(8,128)(2,1)S(1)}, bf16[384,512]{1,0:T(8,128)(2,1)S(1)}, u32[]{:S(2)}, u32[]{:S(2)}) collective-permute-start(bf16[384,512]{1,0:T(8,128)(2,1)S(1)} %collective-permute-done.40.refs_1_), channel_id=1, source_target_pairs={{0,8},{8,0},{1,9},{9,1},{2,10},{10,2},{3,11},{11,3},{4,12},{12,4},... | collective-permute-start | bytes 1179656 | tf_op jit(solution)/shard_map/ppermute | solution.py:36
  177.9 2.9 %collective-permute-start.45 = (bf16[384,512]{1,0:T(8,128)(2,1)S(1)}, bf16[384,512]{1,0:T(8,128)(2,1)S(1)}, u32[]{:S(2)}, u32[]{:S(2)}) collective-permute-start(bf16[384,512]{1,0:T(8,128)(2,1)S(1)} %collective-permute-done.41.refs_2_), channel_id=1, source_target_pairs={{0,8},{8,0},{1,9},{9,1},{2,10},{10,2},{3,11},{11,3},{4,12},{12,4},... | collective-permute-start | bytes 1179656 | tf_op jit(solution)/shard_map/ppermute | solution.py:36
  179.0 1.7 collective-permute-start.46
  (4 other events, 23.7 us)
